TPU v7x, 32 devices: a whole 2x2x4 slice. The times are simulated.
32 devices in a mesh: seq: 4 (over z), dp: 8 (over y, x, core).
Axes of the slice: x: 2, y: 2, z: 4, core: 2. Of those that a mesh axis runs over, the one named last changes fastest.
Arguments:
- layer_input: bfloat16 [8192, 1024], P(('dp', 'seq')), may hold values from -6 to 6
- out_grad: bfloat16 [8192, 1024], P(('dp', 'seq')), may hold values from -6 to 6
- lengths: int32 [8, 3], P('dp'), may hold values from 1 to 682, 1024 in all within a row
- item_owner: int32 [8192, 1], P(('dp', 'seq')), may hold values from 0 to 31; in each aligned block of 256 rows (0 to 255, 256 to 511, ...) at most 16 rows name the same one
- item_row: int32 [8192], P(('dp', 'seq')), may hold values from 0 to 511
- w_attn: bfloat16 [1024, 3072], replicated, may hold values from -0.1875 to 0.1875
- w_gate: bfloat16 [1024, 1024], replicated, may hold values from -0.1875 to 0.1875
- w_out: bfloat16 [1024, 1024], replicated, may hold values from -0.1875 to 0.1875
- emb_table: float32 [16384, 1024], P(('seq', 'dp')), may hold values from -6 to 6
- row_accum: float32 [16384], P(('seq', 'dp')), may hold values from 0.25 to 4
Outputs:
- grad_attn: float32 [1024, 3072], P('dp', 'seq')
- grad_gate: float32 [1024, 1024], P('dp', 'seq')
- grad_out: float32 [1024, 1024], P('dp', 'seq')
- new_table: float32 [16384, 1024], P(('seq', 'dp'))
- new_accum: float32 [16384], P(('seq', 'dp'))
Inputs may be any that keep to these rules, and one draw needn't show every extreme that they name: Each group's 3 lengths sum to 1024; the largest is exactly 682. `item_owner`: among the 256 events of one device at most 16 name one owner, a bound that some block reaches.
All inputs are finite; a program needn't handle non-finite values.
Results may differ from a plain program's by a relative error of at most 0.0092.
Values may be sent and summed in bfloat16 or wider, within the bound.
No kernel may reach another device: no remote copies, remote signals or barrier semaphores. Data moves between devices by JAX's collectives and lax.ppermute only.
A program may use at most 128 MiB of HBM per device.

v0:
```python
import functools

import jax
import jax.numpy as jnp
from jax import lax
from jax.experimental import pallas as pl
from jax.experimental.pallas import tpu as pltpu
from jax.sharding import PartitionSpec as P

D = 1024
H = 16
DH = 64
PAIR = 2 * DH

NORM_EPS = 1e-05
LEARN_RATE = 0.1
VMEM_LIMIT = 56 * 1024 * 1024
BF = jnp.bfloat16
F32 = jnp.float32


def dot_nn(a, b):
    return lax.dot_general(a, b, (((1,), (0,)), ((), ())), preferred_element_type=F32)


def dot_nt(a, b):
    return lax.dot_general(a, b, (((1,), (1,)), ((), ())), preferred_element_type=F32)


def history_start(lengths_ref, users, place):
    start = jnp.zeros_like(place)
    end = jnp.int32(0)
    for user in range(users - 1):
        end = end + lengths_ref[0, user]
        start = jnp.where(place >= end, end, start)
    return start


def head_columns(kind, head):
    first = head // 2 * 4 * PAIR + head % 2 * 3 * DH + kind * DH
    return slice(first, first + DH)


def gate_columns(pair):
    return slice(pair * 4 * PAIR + 3 * PAIR, (pair + 1) * 4 * PAIR)


def forward_kernel(*refs, blk, users, maxlen, count):
    lengths_ref, order_ref = refs[:2]
    x_refs = refs[2 : 2 + count]
    w_ref = refs[2 + count]
    outs = refs[3 + count :]
    if count > 1:
        x_out_ref, outs = outs[0], outs[1:]
    acts_ref, slopes_ref, gate_ref, weights_ref, score_slope_ref, heads_ref = outs
    i = pl.program_id(0)
    heads = weights_ref.shape[0]
    chunks = x_refs[0].shape[0] // blk

    @pl.when(i == 0)
    def _():
        for b in range(count):
            for r in range(chunks):
                at = pl.ds(pl.multiple_of(order_ref[b * chunks + r] * blk, blk), blk)
                x = x_refs[b][r * blk : (r + 1) * blk, :]
                if count > 1:
                    x_out_ref[at, :] = x
                for p in range(heads // 2):
                    lanes = slice(p * 4 * PAIR, (p + 1) * 4 * PAIR)
                    half = 0.5 * dot_nn(x, w_ref[:, lanes])
                    t = jnp.tanh(half)
                    prod = half * t
                    silu = half + prod
                    acts_ref[at, lanes] = silu.astype(BF)
                    gate_ref[at, p * PAIR : (p + 1) * PAIR] = silu[:, 3 * PAIR :]
                    slopes_ref[at, lanes] = (0.5 * (1.0 + t) * (1.0 + half - prod)).astype(BF)

    at_i = pl.ds(pl.multiple_of(i * blk, blk), blk)
    q_half = [acts_ref[at_i, head_columns(1, h)] * jnp.asarray(0.5 * DH**-0.5, BF) for h in range(heads)]
    row = i * blk + lax.broadcasted_iota(jnp.int32, (blk, blk), 0)
    col0 = lax.broadcasted_iota(jnp.int32, (blk, blk), 1)
    start = history_start(lengths_ref, users, row)

    def column(j, acc):
        at_j = pl.ds(pl.multiple_of(j * blk, blk), blk)
        col = col0 + j * blk
        allowed = (col <= row) & (col >= start)
        outs = []
        for h in range(heads):
            half = dot_nt(q_half[h], acts_ref[at_j, head_columns(2, h)])
            half = jnp.where(allowed, half, -64.0)
            t = jnp.tanh(half)
            p = half * t
            weights = (half + p).astype(BF)
            weights_ref[h, :, at_j] = weights
            score_slope_ref[h, :, at_j] = ((1.0 + t) * (1.0 + half - p)).astype(BF)
            outs.append(acc[h] + dot_nn(weights, acts_ref[at_j, head_columns(0, h)]))
        return tuple(outs)

    first = history_start(lengths_ref, users, i * blk) // blk
    zero = jnp.zeros((blk, DH), F32)
    acc = lax.fori_loop(first, i + 1, column, (zero,) * heads)
    heads_ref[...] = (jnp.concatenate(acc, axis=1) * (1.0 / maxlen)).astype(BF)


def forward_attention(lengths, order, x_blocks, w_own, blk, maxlen):
    count = len(x_blocks)
    block_rows = x_blocks[0].shape[0]
    positions = count * block_rows
    cols = w_own.shape[1] // 4
    heads = cols // DH
    users = lengths.shape[1]
    elements = heads * positions * positions // 2
    whole = lambda i: (0, 0)
    out_specs = [
        pl.BlockSpec((positions, 4 * cols), whole),
        pl.BlockSpec((positions, 4 * cols), whole),
        pl.BlockSpec((positions, cols), whole),
        pl.BlockSpec((heads, blk, positions), lambda i: (0, i, 0)),
        pl.BlockSpec((heads, blk, positions), lambda i: (0, i, 0)),
        pl.BlockSpec((blk, cols), lambda i: (i, 0)),
    ]
    out_shape = [
        jax.ShapeDtypeStruct((positions, 4 * cols), BF),
        jax.ShapeDtypeStruct((positions, 4 * cols), BF),
        jax.ShapeDtypeStruct((positions, cols), F32),
        jax.ShapeDtypeStruct((heads, positions, positions), BF),
        jax.ShapeDtypeStruct((heads, positions, positions), BF),
        jax.ShapeDtypeStruct((positions, cols), BF),
    ]
    if count > 1:
        out_specs = [pl.BlockSpec((positions, D), whole)] + out_specs
        out_shape = [jax.ShapeDtypeStruct((positions, D), BF)] + out_shape
    return pl.pallas_call(
        functools.partial(forward_kernel, blk=blk, users=users, maxlen=maxlen, count=count),
        grid=(positions // blk,),
        in_specs=[pl.BlockSpec(memory_space=pltpu.SMEM), pl.BlockSpec(memory_space=pltpu.SMEM)]
        + [pl.BlockSpec((block_rows, D), whole)] * count
        + [pl.BlockSpec((D, 4 * cols), whole)],
        out_specs=out_specs,
        out_shape=out_shape,
        compiler_params=pltpu.CompilerParams(vmem_limit_bytes=VMEM_LIMIT),
        cost_estimate=pl.CostEstimate(
            flops=8 * positions * D * cols + 4 * elements * 256,
            bytes_accessed=4 * positions * D + 4 * elements,
            transcendentals=elements,
        ),
        name="attention_forward",
    )(lengths, order, *x_blocks, w_own)


def stats_kernel(*refs, count):
    order_ref = refs[0]
    mg_refs = refs[1 : 1 + count]
    gate_ref, heads_ref, mg_out_ref, stats_ref = refs[1 + count :]
    rows = mg_refs[0].shape[0]
    for b in range(count):
        at = pl.ds(pl.multiple_of(order_ref[b] * rows, rows), rows)
        mg = mg_refs[b][...]
        mg_out_ref[at, :] = mg
        ng = mg.astype(F32) * gate_ref[at, :]
        heads = heads_ref[at, :].astype(F32)
        mean = jnp.mean(heads, axis=1, keepdims=True)
        centred = heads - mean
        square = jnp.sum(centred * centred, axis=1, keepdims=True)
        total = jnp.sum(ng, axis=1, keepdims=True)
        cross = jnp.sum(ng * centred, axis=1, keepdims=True)
        lane = lax.broadcasted_iota(jnp.int32, (rows, 128), 1)
        packed = jnp.where(lane == 0, mean, jnp.where(lane == 1, square, jnp.where(lane == 2, total, cross)))
        stats_ref[:, at] = jnp.transpose(packed)[:8, :]


def event_stats(order, mg_blocks, gate, heads):
    positions, cols = heads.shape
    count = len(mg_blocks)
    vmem = pl.BlockSpec(memory_space=pltpu.VMEM)
    return pl.pallas_call(
        functools.partial(stats_kernel, count=count),
        in_specs=[pl.BlockSpec(memory_space=pltpu.SMEM)] + [vmem] * (count + 2),
        out_specs=[vmem, vmem],
        out_shape=[
            jax.ShapeDtypeStruct((positions, cols), BF),
            jax.ShapeDtypeStruct((8, positions), F32),
        ],
        compiler_params=pltpu.CompilerParams(vmem_limit_bytes=VMEM_LIMIT),
        cost_estimate=pl.CostEstimate(flops=20 * positions * cols, bytes_accessed=10 * positions * cols, transcendentals=0),
        name="event_stats",
    )(order, *mg_blocks, gate, heads)


def combined_stats(stats_refs, cols):
    shards = len(stats_refs)
    positions = stats_refs[0].shape[1]
    means = [ref[0:1, :] for ref in stats_refs]
    mean = sum(means) * (1.0 / shards)
    square = jnp.zeros_like(mean)
    total = jnp.zeros_like(mean)
    cross = jnp.zeros_like(mean)
    for s, ref in enumerate(stats_refs):
        shift = means[s] - mean
        part = ref[2:3, :]
        square = square + ref[1:2, :] + cols * shift * shift
        total = total + part
        cross = cross + ref[3:4, :] + shift * part
    inv_dev = lax.rsqrt(square * (1.0 / D) + NORM_EPS)
    kind = lax.broadcasted_iota(jnp.int32, (128, positions), 0)
    rest = jnp.where(kind == 2, total * (1.0 / D), cross * inv_dev * (1.0 / D))
    packed = jnp.where(kind == 0, mean, jnp.where(kind == 1, inv_dev, rest))
    per_event = jnp.transpose(packed)
    return [per_event[:, k : k + 1] for k in range(4)]


def backward_kernel(*refs, blk, users, maxlen, shards):
    lengths_ref = refs[0]
    stats_refs = refs[1 : 1 + shards]
    mg_ref, gate_ref, heads_ref, acts_ref, slopes_ref, weights_ref, score_slope_ref = refs[1 + shards : 8 + shards]
    grad_ref, mixed_ref, o_ref, o_t, q_t, vg_t, kg_t, qg = refs[8 + shards :]
    i = pl.program_id(0)
    positions, cols = o_ref.shape
    heads = cols // DH
    blocks = positions // blk
    scale = DH ** (-0.5)

    @pl.when(i == 0)
    def _():
        mean, inv_dev, total, cross = combined_stats(stats_refs, cols)
        for p in range(heads // 2):
            lanes = slice(p * PAIR, (p + 1) * PAIR)
            normed = (heads_ref[:, lanes].astype(F32) - mean) * inv_dev
            gate = gate_ref[:, lanes]
            mg = mg_ref[:, lanes].astype(F32)
            mixed_ref[:, lanes] = (normed * gate).astype(BF)
            gate_slope = slopes_ref[:, gate_columns(p)].astype(F32)
            grad_ref[:, gate_columns(p)] = (mg * normed * gate_slope).astype(BF)
            o_ref[:, lanes] = (inv_dev * (mg * gate - total - normed * cross)).astype(BF)
        o_t[...] = jnp.transpose(o_ref[...])
        queries = [acts_ref[:, head_columns(1, h)] for h in range(heads)]
        q_t[...] = jnp.transpose(jnp.concatenate(queries, axis=1))
        vg_t[...] = jnp.zeros_like(vg_t)
        kg_t[...] = jnp.zeros_like(kg_t)

    at_i = pl.ds(pl.multiple_of(i * blk, blk), blk)

    def column(j, acc):
        at_j = pl.ds(pl.multiple_of(j * blk, blk), blk)
        outs = []
        for h in range(heads):
            lanes = slice(h * DH, (h + 1) * DH)
            weight_grad = dot_nt(o_ref[at_i, lanes], acts_ref[at_j, head_columns(0, h)])
            score_grad = (weight_grad * score_slope_ref[h, :, at_j].astype(F32)).astype(BF)
            vg_t[lanes, at_j] += dot_nn(o_t[lanes, at_i], weights_ref[h, :, at_j])
            kg_t[lanes, at_j] += dot_nn(q_t[lanes, at_i], score_grad)
            outs.append(acc[h] + dot_nn(score_grad, acts_ref[at_j, head_columns(2, h)]))
        return tuple(outs)

    first = history_start(lengths_ref, users, i * blk) // blk
    zero = jnp.zeros((blk, DH), F32)
    acc = lax.fori_loop(first, i + 1, column, (zero,) * heads)
    qg[at_i, :] = jnp.concatenate(acc, axis=1)

    @pl.when(i == blocks - 1)
    def _():
        factor = 0.5 * scale / maxlen
        grads = [jnp.transpose(vg_t[...]) * (1.0 / maxlen), qg[...] * factor, jnp.transpose(kg_t[...]) * factor]
        pieces = [grads[kind][:, h * DH : (h + 1) * DH] for h in range(heads) for kind in range(3)]
        for n in range(3 * heads // 2):
            first_lane = n // 3 * 4 * PAIR + n % 3 * PAIR
            lanes = slice(first_lane, first_lane + PAIR)
            grad = jnp.concatenate(pieces[2 * n : 2 * n + 2], axis=1).astype(BF).astype(F32)
            grad_ref[:, lanes] = (grad * slopes_ref[:, lanes].astype(F32)).astype(BF)


def backward_attention(lengths, stats, mg, gate, head_outs, acts, slopes, weights, score_slope, blk, maxlen):
    positions, cols = mg.shape
    heads = cols // DH
    shards = len(stats)
    users = lengths.shape[1]
    elements = heads * positions * positions // 2
    whole = lambda i: (0, 0)
    return pl.pallas_call(
        functools.partial(backward_kernel, blk=blk, users=users, maxlen=maxlen, shards=shards),
        grid=(positions // blk,),
        in_specs=[pl.BlockSpec(memory_space=pltpu.SMEM)]
        + [pl.BlockSpec((8, positions), whole)] * shards
        + [
            pl.BlockSpec((positions, cols), whole),
            pl.BlockSpec((positions, cols), whole),
            pl.BlockSpec((positions, cols), whole),
            pl.BlockSpec((positions, 4 * cols), whole),
            pl.BlockSpec((positions, 4 * cols), whole),
            pl.BlockSpec((heads, blk, positions), lambda i: (0, i, 0)),
            pl.BlockSpec((heads, blk, positions), lambda i: (0, i, 0)),
        ],
        out_specs=[pl.BlockSpec((positions, 4 * cols), whole), pl.BlockSpec((positions, cols), whole)],
        out_shape=[
            jax.ShapeDtypeStruct((positions, 4 * cols), BF),
            jax.ShapeDtypeStruct((positions, cols), BF),
        ],
        scratch_shapes=[
            pltpu.VMEM((positions, cols), BF),
            pltpu.VMEM((cols, positions), BF),
            pltpu.VMEM((cols, positions), BF),
            pltpu.VMEM((cols, positions), F32),
            pltpu.VMEM((cols, positions), F32),
            pltpu.VMEM((positions, cols), F32),
        ],
        compiler_params=pltpu.CompilerParams(vmem_limit_bytes=VMEM_LIMIT),
        cost_estimate=pl.CostEstimate(
            flops=8 * elements * 256, bytes_accessed=4 * elements + 26 * positions * cols, transcendentals=0
        ),
        name="attention_backward",
    )(lengths, *stats, mg, gate, head_outs, acts, slopes, weights, score_slope)


def update_kernel(ids_ref, rows_ref, table_ref, accum_ref, new_table_ref, new_accum_ref):
    i = pl.program_id(0)
    blk = table_ref.shape[0]
    slots = rows_ref.shape[0]
    row = i * blk + lax.broadcasted_iota(jnp.int32, (blk, slots), 0)
    hits = jnp.where(row == ids_ref[...], 1.0, 0.0).astype(BF)
    grad = dot_nn(hits, rows_ref[...])
    accum = jnp.transpose(jnp.broadcast_to(accum_ref[...], (128, blk)))[:, :1] + jnp.mean(grad * grad, axis=1, keepdims=True)
    new_accum_ref[...] = jnp.transpose(jnp.broadcast_to(accum, (blk, 128)))[:1, :]
    new_table_ref[...] = table_ref[...] - LEARN_RATE * grad * lax.rsqrt(accum)


def update_rows(got_ids, got_rows, emb_table, row_accum):
    rows_own = emb_table.shape[0]
    slots = got_rows.shape[0]
    blk = min(256, rows_own)
    new_table, new_accum = pl.pallas_call(
        update_kernel,
        grid=(rows_own // blk,),
        in_specs=[
            pl.BlockSpec((1, slots), lambda i: (0, 0)),
            pl.BlockSpec((slots, D), lambda i: (0, 0)),
            pl.BlockSpec((blk, D), lambda i: (i, 0)),
            pl.BlockSpec((1, blk), lambda i: (0, i)),
        ],
        out_specs=[
            pl.BlockSpec((blk, D), lambda i: (i, 0)),
            pl.BlockSpec((1, blk), lambda i: (0, i)),
        ],
        out_shape=[
            jax.ShapeDtypeStruct((rows_own, D), F32),
            jax.ShapeDtypeStruct((1, rows_own), F32),
        ],
        compiler_params=pltpu.CompilerParams(vmem_limit_bytes=VMEM_LIMIT),
        cost_estimate=pl.CostEstimate(
            flops=2 * rows_own * slots * D, bytes_accessed=8 * rows_own * D + 2 * slots * D, transcendentals=rows_own
        ),
        name="update_rows",
    )(got_ids.reshape(1, slots), got_rows, emb_table, row_accum.reshape(1, rows_own))
    return new_table, new_accum.reshape(rows_own)


def own_weights(w_attn, w_gate, part, pairs):
    slices = []
    for p in range(pairs):
        at = part * pairs + p
        slices.append(lax.dynamic_slice_in_dim(w_attn, at * 3 * PAIR, 3 * PAIR, 1))
        slices.append(lax.dynamic_slice_in_dim(w_gate, at * PAIR, PAIR, 1))
    return jnp.concatenate(slices, axis=1)


def attn_and_gate(proj, pairs):
    pieces = [proj[:, p * 4 * PAIR : (p + 1) * 4 * PAIR] for p in range(pairs)]
    attn = jnp.concatenate([piece[:, : 3 * PAIR] for piece in pieces], axis=1)
    return attn, jnp.concatenate([piece[:, 3 * PAIR :] for piece in pieces], axis=1)


def row_slots(owners, devices, capacity):
    events = owners.shape[0]
    owner_hits = (owners[:, None] == jnp.arange(devices, dtype=jnp.int32)[None, :]).astype(BF)
    place = jnp.arange(events, dtype=jnp.int32)
    before = (place[:, None] > place[None, :]).astype(BF)
    earlier = jnp.dot(before, owner_hits, preferred_element_type=F32)
    return owners * capacity + jnp.sum(earlier * owner_hits.astype(F32), axis=1).astype(jnp.int32)


def slot_table(flat_slot, slots):
    return jnp.arange(slots, dtype=jnp.int32)[:, None] == flat_slot[None, :]


def to_owners(rows, devices, capacity):
    shape = (devices, capacity) + rows.shape[1:]
    got = lax.all_to_all(rows.reshape(shape), ("seq", "dp"), split_axis=0, concat_axis=0, tiled=True)
    return got.reshape(rows.shape)


def ids_to_owners(flat_slot, item_row, rows_own, devices, capacity):
    filled = slot_table(flat_slot, devices * capacity)
    ids = jnp.min(jnp.where(filled, item_row[None, :], rows_own), axis=1).astype(jnp.int32)
    return to_owners(ids, devices, capacity)


def rows_by_slot(flat_slot, input_grad, slots):
    filled = slot_table(flat_slot, slots).astype(BF)
    return jnp.dot(filled, input_grad.astype(BF), preferred_element_type=F32).astype(BF)


TN = (((0,), (0,)), ((), ()))


def dot_tn(a, b):
    return lax.dot_general(a, b, TN, preferred_element_type=F32)


def body_whole(
    layer_input, out_grad, lengths, item_owner, item_row, w_attn, w_gate, w_out, emb_table, row_accum
):
    seq_count = lax.axis_size("seq")
    dp_count = lax.axis_size("dp")
    devices = seq_count * dp_count
    seq_id = lax.axis_index("seq")
    tokens_dev = layer_input.shape[0]
    positions = tokens_dev * seq_count
    maxlen = 2 * positions // 3
    blk = min(256, positions)
    cols = D // seq_count
    pairs = cols // PAIR
    capacity = max(2, 2 * tokens_dev // devices)

    w_own = own_weights(w_attn, w_gate, seq_id, pairs)
    w_out_own = lax.dynamic_slice_in_dim(w_out, seq_id * cols, cols, 0)
    flat_slot = row_slots(item_owner[:, 0], devices, capacity)
    got_ids = ids_to_owners(flat_slot, item_row, emb_table.shape[0], devices, capacity)

    x_full = lax.all_gather(layer_input, "seq", axis=0, tiled=True)
    og_full = lax.all_gather(out_grad, "seq", axis=0, tiled=True)
    order = jnp.arange(positions // blk, dtype=jnp.int32)
    acts, slopes, gate, weights, score_slope, heads = forward_attention(
        lengths, order, [x_full], w_own, blk, maxlen
    )
    mg = dot_nt(og_full, w_out_own).astype(BF)
    mg, stats_own = event_stats(jnp.zeros((1,), jnp.int32), [mg], gate, heads)
    stats = lax.all_gather(stats_own, "seq", axis=0, tiled=False)
    grads, mixed = backward_attention(
        lengths, [stats[s] for s in range(seq_count)], mg, gate, heads, acts, slopes, weights, score_slope, blk, maxlen
    )

    input_part = dot_nt(grads, w_own).astype(BF)
    got = lax.all_to_all(
        input_part.reshape(seq_count, tokens_dev, D), "seq", split_axis=0, concat_axis=0, tiled=True
    )
    input_grad = jnp.sum(got.astype(F32), axis=0) + out_grad.astype(F32)
    got_rows = to_owners(rows_by_slot(flat_slot, input_grad, devices * capacity), devices, capacity)
    new_table, new_accum = update_rows(got_ids, got_rows, emb_table, row_accum)

    out_part = dot_tn(mixed, og_full).astype(BF)
    share = dp_count // seq_count
    out_part = out_part.reshape(share, D // dp_count, seq_count, cols).transpose(0, 2, 1, 3).reshape(D, cols)
    merged = jnp.concatenate([dot_tn(x_full, grads).astype(BF), out_part], axis=1)
    merged = lax.psum_scatter(merged, "dp", scatter_dimension=0, tiled=True)
    steps = []
    for s in range(seq_count):
        for piece in range(dp_count):
            part, target = divmod(piece, seq_count)
            steps.append((s * dp_count + piece, target * dp_count + s * share + part))
    grad_out = lax.ppermute(merged[:, 4 * cols :], ("seq", "dp"), steps).astype(F32)
    grad_attn, grad_gate = attn_and_gate(merged[:, : 4 * cols].astype(F32), pairs)
    return (grad_attn, grad_gate, grad_out, new_table, new_accum)


SEQ = 4
PLANE = 4


def send(array, target):
    steps = []
    for s in range(SEQ):
        for e in range(PLANE):
            for c in range(2):
                to = target(s, e, c)
                if to is not None:
                    steps.append((s * 2 * PLANE + 2 * e + c, to[0] * 2 * PLANE + 2 * to[1] + to[2]))
    return lax.ppermute(array, ("seq", "dp"), steps)


def home(s, c):
    return c == s // 2


def swap_far(array):
    return send(array, lambda s, e, c: None if home(s, c) else (3 - s, e, 1 - c))


def fetch_near(array):
    return send(array, lambda s, e, c: (s ^ 1, e, c) if home(s, c) else ((3 - s) ^ 1, e, 1 - c))


def swap_near(array):
    return send(array, lambda s, e, c: (s ^ 1, e, c))


def swap_core(array):
    return send(array, lambda s, e, c: (s, e, 1 - c))


def swap_x(array):
    return send(array, lambda s, e, c: (s, e ^ 1, c))


def swap_y(array):
    return send(array, lambda s, e, c: (s, e ^ 2, c))


def tie(*arrays):
    return lax.optimization_barrier(arrays)


def halves(array, bit, axis):
    kept = lax.dynamic_index_in_dim(array, bit, axis, keepdims=False)
    sent = lax.dynamic_index_in_dim(array, 1 - bit, axis, keepdims=False)
    return kept, sent


def body_pairs(
    layer_input, out_grad, lengths, item_owner, item_row, w_attn, w_gate, w_out, emb_table, row_accum
):
    devices = 2 * PLANE * SEQ
    s = lax.axis_index("seq")
    d = lax.axis_index("dp")
    e, c = d // 2, d % 2
    y, x = e // 2, e % 2
    tokens_dev = layer_input.shape[0]
    positions = tokens_dev * SEQ
    maxlen = 2 * positions // 3
    blk = min(256, positions)
    cols = D // SEQ
    pairs = cols // PAIR
    rows_own = emb_table.shape[0]
    capacity = max(2, 2 * tokens_dev // devices)
    at_home = c == s // 2
    part = 2 * (s % 2) + c

    def block_of(seq, core):
        return jnp.where(core == seq // 2, seq, 3 - seq)

    mine_at, near_at = block_of(s, c), block_of(s ^ 1, c)
    core_at, diag_at = block_of(s, 1 - c), block_of(s ^ 1, 1 - c)
    order = jnp.stack([mine_at, near_at, core_at, diag_at]).astype(jnp.int32)

    x_far = swap_far(layer_input)
    x_near = fetch_near(layer_input)
    users = lengths.shape[1]
    flat_slot = row_slots(item_owner[:, 0], devices, capacity)
    small = jnp.concatenate([flat_slot[None, :], jnp.pad(lengths, ((0, 0), (0, 128 - users)))], axis=1)
    small = jnp.where(at_home, small, swap_far(small))
    lengths = small[:, tokens_dev : tokens_dev + users]
    got_ids = ids_to_owners(flat_slot, item_row, rows_own, devices, capacity)
    w_own = own_weights(w_attn, w_gate, part, pairs)
    mg_own = dot_nt(out_grad, w_out).astype(BF)
    mg_sent = [lax.dynamic_slice_in_dim(mg_own, (s + k) % SEQ * cols, cols, 1) for k in range(SEQ)]
    x_far, x_near, w_own, lengths, got_ids, *mg_sent = tie(x_far, x_near, w_own, lengths, got_ids, *mg_sent)
    x_here = jnp.concatenate([jnp.where(at_home, layer_input, x_far), x_near], axis=0)
    x_there = swap_core(x_here)
    x_here, *mg_sent = tie(x_here, *mg_sent)
    mg_blocks = []
    for k, piece in enumerate(mg_sent):
        mg_blocks.append(send(piece, lambda s, e, c: (2 * c + (s + k) % SEQ // 2, e, (s + k) % SEQ % 2)))
    mg_order = jnp.stack([(part - k) % SEQ for k in range(SEQ)]).astype(jnp.int32)

    x_full, acts, slopes, gate, weights, score_slope, heads = forward_attention(
        lengths, order, [x_here, x_there], w_own, blk, maxlen
    )
    heads, *mg_blocks = tie(heads, *mg_blocks)
    mg, stats_own = event_stats(mg_order, mg_blocks, gate, heads)
    stats = [
        stats_own,
        swap_core(stats_own),
        swap_near(stats_own),
        send(stats_own, lambda s, e, c: (s ^ 1, e, 1 - c)),
    ]
    *stats, og_own = tie(*stats, out_grad)
    og_far = swap_far(og_own)
    og_near = fetch_near(og_own)
    grads, mixed = backward_attention(
        lengths, stats, mg, gate, heads, acts, slopes, weights, score_slope, blk, maxlen
    )

    def input_part(grads, block, columns=slice(None)):
        return dot_nt(lax.dynamic_slice_in_dim(grads, block * tokens_dev, tokens_dev, 0), w_own[columns])

    og_far, og_near, grads = tie(og_far, og_near, grads)
    from_diag, near_sums, from_near = [], [], []
    column_halves = (slice(0, D // 2), slice(D // 2, D))
    for columns in column_halves:
        from_diag.append(swap_core(input_part(grads, diag_at, columns).astype(BF)))
    for columns, got in zip(column_halves, from_diag):
        near_sums.append((input_part(grads, near_at, columns) + got.astype(F32)).astype(BF))
        from_near.append(swap_near(near_sums[-1]))
    *near_sums, grads, og_far, og_near = tie(*near_sums, grads, og_far, og_near)
    core_part = input_part(grads, core_at).astype(BF)
    from_core = swap_core(core_part)
    og_mine = jnp.where(at_home, out_grad, og_far)
    input_grad = input_part(grads, mine_at) + og_mine.astype(F32)

    core_part, grads, mixed = tie(core_part, grads, mixed)
    half = 5 * cols // 2
    rest = 4 * cols - half
    proj = dot_tn(x_full, grads).astype(BF).reshape(2, 2, D // PLANE, 4 * cols)
    a_kept, a_sent = halves(proj[..., :half], x, 1)
    b_kept, b_sent = halves(proj[..., half:], y, 0)
    a_got = swap_x(a_sent)
    og_here = jnp.concatenate([og_mine, og_near], axis=0)
    og_there = swap_core(og_here)
    a_sent, mixed = tie(a_sent, mixed)
    mixed_rows = [lax.dynamic_slice_in_dim(mixed, at * tokens_dev, tokens_dev, 0) for at in (mine_at, near_at, core_at, diag_at)]
    out_part = dot_tn(jnp.concatenate(mixed_rows[:2], axis=0), og_here)
    out_part = (out_part + dot_tn(jnp.concatenate(mixed_rows[2:], axis=0), og_there)).astype(BF)

    def picked(bit, low, high):
        return jnp.where(bit == 0, low, high)

    def b_message(rows, out):
        return jnp.concatenate([rows[0], rows[1], out], axis=1)

    low, high = out_part[:, : D // 2], out_part[:, D // 2 :]
    b_kept = b_message(b_kept, picked(y, low, high))
    b_sent = b_message(b_sent, picked(y, high, low))
    b_got = swap_y(b_sent)

    input_grad = input_grad + from_core.astype(F32) + jnp.concatenate(from_near, axis=1).astype(F32)
    got_rows = to_owners(rows_by_slot(small[0, :tokens_dev], input_grad, devices * capacity), devices, capacity)

    a = (a_kept.astype(F32) + a_got.astype(F32)).astype(BF)
    a_kept, a_sent = halves(a, y, 0)
    a_got = swap_y(a_sent)
    b = (b_kept.astype(F32) + b_got.astype(F32)).astype(BF)
    b0 = jnp.concatenate([b[:, :rest], b[:, 2 * rest : 2 * rest + cols]], axis=1)
    b1 = jnp.concatenate([b[:, rest : 2 * rest], b[:, 2 * rest + cols :]], axis=1)
    b_got = swap_x(picked(x, b1, b0))
    a = (a_kept.astype(F32) + a_got.astype(F32)).astype(BF)
    b = (picked(x, b0, b1).astype(F32) + b_got.astype(F32)).astype(BF)

    def last(array, target):
        pieces = array.reshape(2, D // (2 * PLANE), array.shape[1])
        one, other = halves(pieces, s // 2, 0)
        one = send(one, lambda s, e, c: target(s, e, c, s // 2))
        return one, send(other, lambda s, e, c: target(s, e, c, 1 - s // 2))

    proj = last(jnp.concatenate([a, b[:, :rest]], axis=1), lambda s, e, c, piece: (2 * (s % 2) + c, e, piece))
    out = last(b[:, rest:], lambda s, e, c, piece: (e, 2 * (s % 2) + c, piece))
    ids = got_ids.reshape(SEQ, PLANE, 2, capacity)
    at_seq = jnp.arange(SEQ, dtype=jnp.int32)[:, None, None, None]
    at_core = jnp.arange(2, dtype=jnp.int32)[None, None, :, None]
    ids = jnp.where(at_core == at_seq // 2, ids, ids[::-1, :, ::-1])
    new_table, new_accum = update_rows(ids, got_rows, emb_table, row_accum)
    *proj, new_accum = tie(*proj, new_accum)
    grad_attn, grad_gate = attn_and_gate(proj[0].astype(F32) + proj[1].astype(F32), pairs)
    return (grad_attn, grad_gate, out[0].astype(F32) + out[1].astype(F32), new_table, new_accum)


def solution(mesh):
    placed = (
        P(("dp", "seq"), None),
        P(("dp", "seq"), None),
        P("dp", None),
        P(("dp", "seq"), None),
        P(("dp", "seq")),
        P(),
        P(),
        P(),
        P(("seq", "dp"), None),
        P(("seq", "dp")),
    )
    paired = mesh.shape["seq"] == SEQ and mesh.shape["dp"] == 2 * PLANE
    return jax.shard_map(
        body_pairs if paired else body_whole,
        mesh=mesh,
        in_specs=placed,
        out_specs=(
            P("dp", "seq"),
            P("dp", "seq"),
            P("dp", "seq"),
            P(("seq", "dp"), None),
            P(("seq", "dp")),
        ),
        check_vma=False,
    )
```

profile of v0, /device:TPU:0, one launch (start us, length us, event | category | flops | bytes accessed | tf_op | source)
XLA Modules:
  0.0 183.4 jit_solution(16302068638384646616)
XLA Ops:
  1.5 3.1 %collective-permute-start.1 = (bf16[256,1024]{1,0:T(8,128)(2,1)}, bf16[256,1024]{1,0:T(8,128)(2,1)S(1)}, u32[]{:S(2)}, u32[]{:S(2)}) collective-permute-start(bf16[256,1024]{1,0:T(8,128)(2,1)} %param.10), channel_id=1, source_target_pairs={{0,8},{1,16},{2,10},{3,18},{4,12},{5,20},{6,14},{7,22},{8,0},{9,24... | collective-permute-start | bytes 1572872 | tf_op jit(solution)/shard_map/ppermute | solution.py:477
  9.8 10.3 %all-to-all-start = ((s32[32,1,16]{2,1,0:T(1,128)}), s32[32,1,16]{2,1,0:T(1,128)S(1)}, u32[]{:S(2)}, u32[]{:S(2)}) async-start(s32[32,1,16]{2,1,0:T(1,128)} %bitcast.3), calls=%async_computation | async-start | bytes 32768 | tf_op jit(solution)/shard_map/all_to_all | solution.py:387
  20.2 1.8 convolution_convert_fusion.3
  22.0 1.5 constant_dynamic-slice_fusion.11
  24.6 1.6 pad_maximum_fusion.refs_4_
  26.9 6.3 %all-to-all-done = s32[32,1,16]{2,1,0:T(1,128)S(1)} async-done(((s32[32,1,16]{2,1,0:T(1,128)}), s32[32,1,16]{2,1,0:T(1,128)S(1)}, u32[]{:S(2)}, u32[]{:S(2)}) %all-to-all-start) | async-done | bytes 2080 | tf_op jit(solution)/shard_map/all_to_all | solution.py:387
  36.1 4.7 %collective-permute-start.5 = (bf16[256,256]{1,0:T(8,128)(2,1)S(1)}, bf16[256,256]{1,0:T(8,128)(2,1)S(1)}, u32[]{:S(2)}, u32[]{:S(2)}) collective-permute-start(bf16[256,256]{1,0:T(8,128)(2,1)S(1)} %get-tuple-element.66), channel_id=1, source_target_pairs={{0,1},{1,17},{2,3},{3,19},{4,5},{5,21},{6,7},{7,23},{8,8},{9,24},{... | collective-permute-start | bytes 393224 | tf_op jit(solution)/shard_map/ppermute | solution.py:477
  40.9 3.9 %collective-permute-start.7 = (bf16[256,256]{1,0:T(8,128)(2,1)S(1)}, bf16[256,256]{1,0:T(8,128)(2,1)S(1)}, u32[]{:S(2)}, u32[]{:S(2)}) collective-permute-start(bf16[256,256]{1,0:T(8,128)(2,1)S(1)} %get-tuple-element.68), channel_id=1, source_target_pairs={{0,9},{1,25},{2,11},{3,27},{4,13},{5,29},{6,15},{7,31},{8,0},{9,16... | collective-permute-start | bytes 393224 | tf_op jit(solution)/shard_map/ppermute | solution.py:477
  45.7 20.0 %attention_forward.1 = (bf16[1024,1024]{1,0:T(8,128)(2,1)}, bf16[1024,1024]{1,0:T(8,128)(2,1)}, bf16[1024,1024]{1,0:T(8,128)(2,1)}, f32[1024,256]{1,0:T(8,128)},...) custom-call(s32[1,3]{1,0:T(1,128)} %slice.100.refs_0_, ...), custom_call_target="tpu_custom_call" | custom-call | flops 4294967296 | bytes 12582912 | tf_op jit(solution)/shard_map/attention_forward/pallas_call | solution.py:134
  66.6 3.2 %event_stats.1 = (bf16[1024,256]{1,0:T(8,128)(2,1)}, f32[8,1024]{1,0:T(8,128)}) custom-call(s32[4]{0:T(128)} %get-tuple-element.134.refs_0_, bf16[256,256]{1,0:T(8,128)(2,1)} %copy-done.12, bf16[256,256]{1,0:T(8,128)(2,1)} %copy-done.13, bf16[256,256]{1,0:T(8,128)(2,1)} %copy-done.14, bf16[256,256]{1,0:T(8,128)(2,1)} %copy-done.15, ...), custom_call_target="tpu_custom_call" | custom-call | flops 5242880 | bytes 2621440 | tf_op jit(solution)/shard_map/event_stats/pallas_call | solution.py:177
  71.9 1.4 collective-permute-done.10.refs_4_
  73.3 1.8 collective-permute-done.9.refs_3_
  77.0 19.1 %attention_backward.1 = (bf16[1024,1024]{1,0:T(8,128)(2,1)}, bf16[1024,256]{1,0:T(8,128)(2,1)}) custom-call(s32[1,3]{1,0:T(1,128)} %slice.100.refs_0_, f32[8,1024]{1,0:T(8,128)} %get-tuple-element.77.refs_1_, f32[8,1024]{1,0:T(8,128)} %copy-done.17, f32[8,1024]{1,0:T(8,128)} %copy-done.18, f32[8,1024]{1,0:T(8,128)} %copy-done.16, ...), custom_call_target="tpu_custom_call" | custom-call | flops 4294967296 | bytes 15204352 | tf_op jit(solution)/shard_map/attention_backward/pallas_call | solution.py:280
  96.1 2.2 %convolution_convert_fusion.4 = bf16[256,512]{1,0:T(8,128)(2,1)} fusion(bf16[1024,1024]{1,0:T(8,128)(2,1)S(1)} %copy-done.3, bf16[1024,1024]{1,0:T(8,128)(2,1)} %get-tuple-element.92, s32[]{:T(128)S(6)} %select_n.238), kind=kOutput, calls=%fused_computation.18 | convolution fusion | flops 268566528 | bytes 1835012 | tf_op jit(solution)/shard_map/dot_general | solution.py:27
  98.4 6.1 %collective-permute-start.14 = (bf16[256,512]{1,0:T(8,128)(2,1)}, bf16[256,512]{1,0:T(8,128)(2,1)S(1)}, u32[]{:S(2)}, u32[]{:S(2)}) collective-permute-start(bf16[256,512]{1,0:T(8,128)(2,1)} %convolution_convert_fusion.4), channel_id=1, source_target_pairs={{0,1},{1,0},{2,3},{3,2},{4,5},{5,4},{6,7},{7,6},{8,9},{9,8},{10,11... | collective-permute-start | bytes 786440 | tf_op jit(solution)/shard_map/ppermute | solution.py:477
  104.7 1.7 convolution_convert_fusion.5
  108.5 1.3 pad_maximum_fusion.2
  111.4 2.4 %convolution_convert_fusion = bf16[1024,1024]{1,0:T(8,128)(2,1)S(1)} fusion(bf16[1024,1024]{1,0:T(8,128)(2,1)S(1)} %copy-done.26, bf16[1024,1024]{1,0:T(8,128)(2,1)S(1)} %copy-done.21), kind=kOutput, calls=%fused_computation.1 | convolution fusion | flops 2148532224 | bytes 6291456 | tf_op jit(solution)/shard_map/dot_general | solution.py:406
  114.3 2.1 %collective-permute-start.23 = (bf16[256,512]{1,0:T(8,128)(2,1)S(1)}, bf16[256,512]{1,0:T(8,128)(2,1)S(1)}, u32[]{:S(2)}, u32[]{:S(2)}) collective-permute-start(bf16[256,512]{1,0:T(8,128)(2,1)S(1)} %fusion.5), channel_id=1, source_target_pairs={{0,8},{1,9},{2,10},{3,11},{4,12},{5,13},{6,14},{7,15},{8,0},{9,1},... | collective-permute-start | bytes 786440 | tf_op jit(solution)/shard_map/ppermute | solution.py:477
  118.2 1.5 fusion.26
  121.8 2.1 %collective-permute-start.18 = (bf16[256,1280]{1,0:T(8,128)(2,1)}, bf16[256,1280]{1,0:T(8,128)(2,1)}, u32[]{:S(2)}, u32[]{:S(2)}) collective-permute-start(bf16[256,1280]{1,0:T(8,128)(2,1)} %pad_maximum_fusion.3), channel_id=1, source_target_pairs={{0,4},{1,5},{2,6},{3,7},{4,0},{5,1},{6,2},{7,3},{8,12},{9,13},{10,... | collective-permute-start | bytes 1966088 | tf_op jit(solution)/shard_map/ppermute | solution.py:477
  123.9 4.6 %collective-permute-done.23 = bf16[256,512]{1,0:T(8,128)(2,1)S(1)} collective-permute-done((bf16[256,512]{1,0:T(8,128)(2,1)S(1)}, bf16[256,512]{1,0:T(8,128)(2,1)S(1)}, u32[]{:S(2)}, u32[]{:S(2)}) %collective-permute-start.23) | collective-permute-done | bytes 262176 | tf_op jit(solution)/shard_map/ppermute | solution.py:477
  130.0 3.7 %convolution_convert_fusion.1 = bf16[512,1024]{1,0:T(8,128)(2,1)} fusion(bf16[1024,1024]{1,0:T(8,128)(2,1)S(1)} %copy-done.3, bf16[256,1024]{1,0:T(8,128)(2,1)} %copy-done.23, bf16[256,1024]{1,0:T(8,128)(2,1)} %copy-done.4, bf16[256,512]{1,0:T(8,128)(2,1)} %copy-done.24, bf16[256,512]{1,0:T(8,128)(2,1)} %copy-done.25, ...), kind=kOutput, calls=%fused_computation.2 | convolution fusion | flops 808583168 | bytes 5243908 | tf_op jit(solution)/shard_map/dot_general | solution.py:399
  133.7 4.0 %all-to-all-start.1 = ((bf16[32,16,1024]{2,1,0:T(8,128)(2,1)}), bf16[32,16,1024]{2,1,0:T(8,128)(2,1)S(1)}, u32[]{:S(2)}, u32[]{:S(2)}) async-start(bf16[32,16,1024]{2,1,0:T(8,128)(2,1)} %bitcast.58), calls=%async_computation.1 | async-start | bytes 2097152 | tf_op jit(solution)/shard_map/all_to_all | solution.py:387
  139.1 1.8 %collective-permute-start.16 = (bf16[256,640]{1,0:T(8,128)(2,1)S(1)}, bf16[256,640]{1,0:T(8,128)(2,1)S(1)}, u32[]{:S(2)}, u32[]{:S(2)}) collective-permute-start(bf16[256,640]{1,0:T(8,128)(2,1)S(1)} %dynamic-slice_bitcast_fusion.1), channel_id=1, source_target_pairs={{0,4},{1,5},{2,6},{3,7},{4,0},{5,1},{6,2},{7,3},{8,12},{9,13},{10,... | collective-permute-start | bytes 983048 | tf_op jit(solution)/shard_map/ppermute | solution.py:477
  142.4 1.5 collective-permute-start.19
  144.6 12.4 %collective-permute-done.16 = bf16[256,640]{1,0:T(8,128)(2,1)S(1)} collective-permute-done((bf16[256,640]{1,0:T(8,128)(2,1)S(1)}, bf16[256,640]{1,0:T(8,128)(2,1)S(1)}, u32[]{:S(2)}, u32[]{:S(2)}) %collective-permute-start.16) | collective-permute-done | bytes 327712 | tf_op jit(solution)/shard_map/ppermute | solution.py:477
  159.6 2.7 %collective-permute-start.26 = (bf16[128,256]{1,0:T(8,128)(2,1)S(1)}, bf16[128,256]{1,0:T(8,128)(2,1)S(1)}, u32[]{:S(2)}, u32[]{:S(2)}) collective-permute-start(bf16[128,256]{1,0:T(8,128)(2,1)S(1)} %get-tuple-element.132), channel_id=1, source_target_pairs={{0,1},{1,3},{2,9},{3,11},{4,17},{5,19},{6,25},{7,27},{8,5},{9,7},{... | collective-permute-start | bytes 196616 | tf_op jit(solution)/shard_map/ppermute | solution.py:477
  163.1 3.6 %collective-permute-start.20 = (bf16[128,1024]{1,0:T(8,128)(2,1)}, bf16[128,1024]{1,0:T(8,128)(2,1)}, u32[]{:S(2)}, u32[]{:S(2)}) collective-permute-start(bf16[128,1024]{1,0:T(8,128)(2,1)} %get-tuple-element.120), channel_id=1, source_target_pairs={{0,0},{1,8},{2,2},{3,10},{4,4},{5,12},{6,6},{7,14},{8,16},{9,24},{... | collective-permute-start | bytes 786440 | tf_op jit(solution)/shard_map/ppermute | solution.py:477
  166.7 2.7 %collective-permute-start.21 = (bf16[128,1024]{1,0:T(8,128)(2,1)S(1)}, bf16[128,1024]{1,0:T(8,128)(2,1)}, u32[]{:S(2)}, u32[]{:S(2)}) collective-permute-start(bf16[128,1024]{1,0:T(8,128)(2,1)S(1)} %get-tuple-element.119), channel_id=1, source_target_pairs={{0,1},{1,9},{2,3},{3,11},{4,5},{5,13},{6,7},{7,15},{8,17},{9,25},{... | collective-permute-start | bytes 786440 | tf_op jit(solution)/shard_map/ppermute | solution.py:477
  171.1 4.2 %update_rows.1 = (f32[512,1024]{1,0:T(8,128)}, f32[1,512]{1,0:T(1,128)}) custom-call(s32[1,512]{1,0:T(1,128)} %reshape.148.ids_ref, bf16[512,1024]{1,0:T(8,128)(2,1)} %bitcast.54, f32[512,1024]{1,0:T(8,128)} %table_ref.1, f32[1,512]{1,0:T(1,128)} %bitcast.64), custom_call_target="tpu_custom_call" | custom-call | flops 536870912 | bytes 5242880 | tf_op jit(solution)/shard_map/update_rows/pallas_call | solution.py:331
  175.3 5.4 %collective-permute-done.21 = bf16[128,1024]{1,0:T(8,128)(2,1)} collective-permute-done((bf16[128,1024]{1,0:T(8,128)(2,1)S(1)}, bf16[128,1024]{1,0:T(8,128)(2,1)}, u32[]{:S(2)}, u32[]{:S(2)}) %collective-permute-start.21) | collective-permute-done | bytes 262176 | tf_op jit(solution)/shard_map/ppermute | solution.py:477
  (149 shorter events, 37.1 us)
Async XLA Ops:
  0.6 19.5 %copy-start = (bf16[1024,1024]{1,0:T(8,128)(2,1)S(1)}, bf16[1024,1024]{1,0:T(8,128)(2,1)}, u32[]{:S(2)}) copy-start(bf16[1024,1024]{1,0:T(8,128)(2,1)} %param.17) | copy-start | bytes 6291460
  0.6 33.8 %collective-permute-start = (bf16[256,1024]{1,0:T(8,128)(2,1)}, bf16[256,1024]{1,0:T(8,128)(2,1)S(1)}, u32[]{:S(2)}, u32[]{:S(2)}) collective-permute-start(bf16[256,1024]{1,0:T(8,128)(2,1)} %param.10), channel_id=1, source_target_pairs={{1,24},{3,26},{5,28},{7,30},{9,16},{11,18},{13,20},{15,22},{16,9},... | collective-permute-start | bytes 1572872 | tf_op jit(solution)/shard_map/ppermute | solution.py:477
  1.5 33.0 %collective-permute-start.1 = (bf16[256,1024]{1,0:T(8,128)(2,1)}, bf16[256,1024]{1,0:T(8,128)(2,1)S(1)}, u32[]{:S(2)}, u32[]{:S(2)}) collective-permute-start(bf16[256,1024]{1,0:T(8,128)(2,1)} %param.10), channel_id=1, source_target_pairs={{0,8},{1,16},{2,10},{3,18},{4,12},{5,20},{6,14},{7,22},{8,0},{9,24... | collective-permute-start | bytes 1572872 | tf_op jit(solution)/shard_map/ppermute | solution.py:477
  6.9 19.5 %collective-permute-start.2 = (s32[1,384]{1,0:T(1,128)S(1)}, s32[1,384]{1,0:T(1,128)S(1)}, u32[]{:S(2)}, u32[]{:S(2)}) collective-permute-start(s32[1,384]{1,0:T(1,128)S(1)} %pad_add_fusion), channel_id=1, source_target_pairs={{1,24},{3,26},{5,28},{7,30},{9,16},{11,18},{13,20},{15,22},{16,9},... | collective-permute-start | bytes 4616 | tf_op jit(solution)/shard_map/ppermute | solution.py:477
  9.8 23.4 %all-to-all-start = ((s32[32,1,16]{2,1,0:T(1,128)}), s32[32,1,16]{2,1,0:T(1,128)S(1)}, u32[]{:S(2)}, u32[]{:S(2)}) async-start(s32[32,1,16]{2,1,0:T(1,128)} %bitcast.3), calls=%async_computation | async-start | bytes 32768 | tf_op jit(solution)/shard_map/all_to_all | solution.py:387
  26.4 78.1 %copy-start.19 = (s32[1,384]{1,0:T(1,128)}, s32[1,384]{1,0:T(1,128)S(1)}, u32[]{:S(2)}) copy-start(s32[1,384]{1,0:T(1,128)S(1)} %broadcast_select_fusion.6) | copy-start | bytes 4612
  34.6 10.1 %collective-permute-start.3 = (bf16[512,1024]{1,0:T(8,128)(2,1)S(1)}, bf16[512,1024]{1,0:T(8,128)(2,1)S(1)}, u32[]{:S(2)}, u32[]{:S(2)}) collective-permute-start(bf16[512,1024]{1,0:T(8,128)(2,1)S(1)} %pad_maximum_fusion.1.refs_2_), channel_id=1, source_target_pairs={{0,1},{1,0},{2,3},{3,2},{4,5},{5,4},{6,7},{7,6},{8,9},{9,8},{10,11... | collective-permute-start | bytes 3145736 | tf_op jit(solution)/shard_map/ppermute | solution.py:477
  35.5 30.3 %collective-permute-start.4 = (bf16[256,256]{1,0:T(8,128)(2,1)S(1)}, bf16[256,256]{1,0:T(8,128)(2,1)S(1)}, u32[]{:S(2)}, u32[]{:S(2)}) collective-permute-start(bf16[256,256]{1,0:T(8,128)(2,1)S(1)} %get-tuple-element.65), channel_id=1, source_target_pairs={{0,0},{1,16},{2,2},{3,18},{4,4},{5,20},{6,6},{7,22},{8,1},{9,17},{... | collective-permute-start | bytes 393224 | tf_op jit(solution)/shard_map/ppermute | solution.py:477
  36.1 29.7 %collective-permute-start.5 = (bf16[256,256]{1,0:T(8,128)(2,1)S(1)}, bf16[256,256]{1,0:T(8,128)(2,1)S(1)}, u32[]{:S(2)}, u32[]{:S(2)}) collective-permute-start(bf16[256,256]{1,0:T(8,128)(2,1)S(1)} %get-tuple-element.66), channel_id=1, source_target_pairs={{0,1},{1,17},{2,3},{3,19},{4,5},{5,21},{6,7},{7,23},{8,8},{9,24},{... | collective-permute-start | bytes 393224 | tf_op jit(solution)/shard_map/ppermute | solution.py:477
  40.8 25.0 %collective-permute-start.6 = (bf16[256,256]{1,0:T(8,128)(2,1)S(1)}, bf16[256,256]{1,0:T(8,128)(2,1)S(1)}, u32[]{:S(2)}, u32[]{:S(2)}) collective-permute-start(bf16[256,256]{1,0:T(8,128)(2,1)S(1)} %get-tuple-element.67), channel_id=1, source_target_pairs={{0,8},{1,24},{2,10},{3,26},{4,12},{5,28},{6,14},{7,30},{8,9},{9,25... | collective-permute-start | bytes 393224 | tf_op jit(solution)/shard_map/ppermute | solution.py:477
  40.9 25.0 %collective-permute-start.7 = (bf16[256,256]{1,0:T(8,128)(2,1)S(1)}, bf16[256,256]{1,0:T(8,128)(2,1)S(1)}, u32[]{:S(2)}, u32[]{:S(2)}) collective-permute-start(bf16[256,256]{1,0:T(8,128)(2,1)S(1)} %get-tuple-element.68), channel_id=1, source_target_pairs={{0,9},{1,25},{2,11},{3,27},{4,13},{5,29},{6,15},{7,31},{8,0},{9,16... | collective-permute-start | bytes 393224 | tf_op jit(solution)/shard_map/ppermute | solution.py:477
  69.8 3.6 %collective-permute-start.10 = (f32[8,1024]{1,0:T(8,128)}, f32[8,1024]{1,0:T(8,128)S(1)}, u32[]{:S(2)}, u32[]{:S(2)}) collective-permute-start(f32[8,1024]{1,0:T(8,128)} %get-tuple-element.77.refs_1_), channel_id=1, source_target_pairs={{0,9},{1,8},{2,11},{3,10},{4,13},{5,12},{6,15},{7,14},{8,1},{9,0},... | collective-permute-start | bytes 98312 | tf_op jit(solution)/shard_map/ppermute | solution.py:477
  71.0 2.3 %collective-permute-start.8 = (f32[8,1024]{1,0:T(8,128)}, f32[8,1024]{1,0:T(8,128)S(1)}, u32[]{:S(2)}, u32[]{:S(2)}) collective-permute-start(f32[8,1024]{1,0:T(8,128)} %get-tuple-element.77.refs_1_), channel_id=1, source_target_pairs={{0,1},{1,0},{2,3},{3,2},{4,5},{5,4},{6,7},{7,6},{8,9},{9,8},{10,11... | collective-permute-start | bytes 98312 | tf_op jit(solution)/shard_map/ppermute | solution.py:477
  71.0 4.1 %collective-permute-start.9 = (f32[8,1024]{1,0:T(8,128)}, f32[8,1024]{1,0:T(8,128)S(1)}, u32[]{:S(2)}, u32[]{:S(2)}) collective-permute-start(f32[8,1024]{1,0:T(8,128)} %get-tuple-element.77.refs_1_), channel_id=1, source_target_pairs={{0,8},{1,9},{2,10},{3,11},{4,12},{5,13},{6,14},{7,15},{8,0},{9,1},... | collective-permute-start | bytes 98312 | tf_op jit(solution)/shard_map/ppermute | solution.py:477
  75.1 21.0 %collective-permute-start.11 = (bf16[256,1024]{1,0:T(8,128)(2,1)S(1)}, bf16[256,1024]{1,0:T(8,128)(2,1)S(1)}, u32[]{:S(2)}, u32[]{:S(2)}) collective-permute-start(bf16[256,1024]{1,0:T(8,128)(2,1)S(1)} %copy-done.10), channel_id=1, source_target_pairs={{1,24},{3,26},{5,28},{7,30},{9,16},{11,18},{13,20},{15,22},{16,9},... | collective-permute-start | bytes 1572872 | tf_op jit(solution)/shard_map/ppermute | solution.py:477
  76.0 20.1 %collective-permute-start.12 = (bf16[256,1024]{1,0:T(8,128)(2,1)S(1)}, bf16[256,1024]{1,0:T(8,128)(2,1)}, u32[]{:S(2)}, u32[]{:S(2)}) collective-permute-start(bf16[256,1024]{1,0:T(8,128)(2,1)S(1)} %copy-done.10), channel_id=1, source_target_pairs={{0,8},{1,16},{2,10},{3,18},{4,12},{5,20},{6,14},{7,22},{8,0},{9,24... | collective-permute-start | bytes 1572872 | tf_op jit(solution)/shard_map/ppermute | solution.py:477
  77.0 19.1 %copy-start.3 = (bf16[1024,1024]{1,0:T(8,128)(2,1)S(1)}, bf16[1024,1024]{1,0:T(8,128)(2,1)}, u32[]{:S(2)}) copy-start(bf16[1024,1024]{1,0:T(8,128)(2,1)} %pad_maximum_fusion.refs_4_) | copy-start | bytes 6291460
  98.4 8.1 %collective-permute-start.14 = (bf16[256,512]{1,0:T(8,128)(2,1)}, bf16[256,512]{1,0:T(8,128)(2,1)S(1)}, u32[]{:S(2)}, u32[]{:S(2)}) collective-permute-start(bf16[256,512]{1,0:T(8,128)(2,1)} %convolution_convert_fusion.4), channel_id=1, source_target_pairs={{0,1},{1,0},{2,3},{3,2},{4,5},{5,4},{6,7},{7,6},{8,9},{9,8},{10,11... | collective-permute-start | bytes 786440 | tf_op jit(solution)/shard_map/ppermute | solution.py:477
  106.3 1.6 collective-permute-start.13
  109.8 9.9 %collective-permute-start.17 = (bf16[512,1024]{1,0:T(8,128)(2,1)S(1)}, bf16[512,1024]{1,0:T(8,128)(2,1)S(1)}, u32[]{:S(2)}, u32[]{:S(2)}) collective-permute-start(bf16[512,1024]{1,0:T(8,128)(2,1)S(1)} %pad_maximum_fusion.2), channel_id=1, source_target_pairs={{0,1},{1,0},{2,3},{3,2},{4,5},{5,4},{6,7},{7,6},{8,9},{9,8},{10,11... | collective-permute-start | bytes 3145736 | tf_op jit(solution)/shard_map/ppermute | solution.py:477
  114.1 14.4 %collective-permute-start.22 = (bf16[256,1024]{1,0:T(8,128)(2,1)S(1)}, bf16[256,1024]{1,0:T(8,128)(2,1)S(1)}, u32[]{:S(2)}, u32[]{:S(2)}) collective-permute-start(bf16[256,1024]{1,0:T(8,128)(2,1)S(1)} %convolution_convert_fusion.2), channel_id=1, source_target_pairs={{0,1},{1,0},{2,3},{3,2},{4,5},{5,4},{6,7},{7,6},{8,9},{9,8},{10,11... | collective-permute-start | bytes 1572872 | tf_op jit(solution)/shard_map/ppermute | solution.py:477
  114.3 9.6 %collective-permute-start.24 = (bf16[256,512]{1,0:T(8,128)(2,1)S(1)}, bf16[256,512]{1,0:T(8,128)(2,1)S(1)}, u32[]{:S(2)}, u32[]{:S(2)}) collective-permute-start(bf16[256,512]{1,0:T(8,128)(2,1)S(1)} %fusion.6), channel_id=1, source_target_pairs={{0,8},{1,9},{2,10},{3,11},{4,12},{5,13},{6,14},{7,15},{8,0},{9,1},... | collective-permute-start | bytes 786440 | tf_op jit(solution)/shard_map/ppermute | solution.py:477
  114.3 14.2 %collective-permute-start.23 = (bf16[256,512]{1,0:T(8,128)(2,1)S(1)}, bf16[256,512]{1,0:T(8,128)(2,1)S(1)}, u32[]{:S(2)}, u32[]{:S(2)}) collective-permute-start(bf16[256,512]{1,0:T(8,128)(2,1)S(1)} %fusion.5), channel_id=1, source_target_pairs={{0,8},{1,9},{2,10},{3,11},{4,12},{5,13},{6,14},{7,15},{8,0},{9,1},... | collective-permute-start | bytes 786440 | tf_op jit(solution)/shard_map/ppermute | solution.py:477
  117.3 20.4 %collective-permute-start.15 = (bf16[2,256,640]{2,1,0:T(8,128)(2,1)}, bf16[2,256,640]{2,1,0:T(8,128)(2,1)}, u32[]{:S(2)}, u32[]{:S(2)}) collective-permute-start(bf16[2,256,640]{2,1,0:T(8,128)(2,1)} %dynamic-slice_bitcast_fusion), channel_id=1, source_target_pairs={{0,2},{1,3},{2,0},{3,1},{4,6},{5,7},{6,4},{7,5},{8,10},{9,11},{10,... | collective-permute-start | bytes 1966088 | tf_op jit(solution)/shard_map/ppermute | solution.py:477
  121.8 19.1 %collective-permute-start.18 = (bf16[256,1280]{1,0:T(8,128)(2,1)}, bf16[256,1280]{1,0:T(8,128)(2,1)}, u32[]{:S(2)}, u32[]{:S(2)}) collective-permute-start(bf16[256,1280]{1,0:T(8,128)(2,1)} %pad_maximum_fusion.3), channel_id=1, source_target_pairs={{0,4},{1,5},{2,6},{3,7},{4,0},{5,1},{6,2},{7,3},{8,12},{9,13},{10,... | collective-permute-start | bytes 1966088 | tf_op jit(solution)/shard_map/ppermute | solution.py:477
  133.7 36.4 %all-to-all-start.1 = ((bf16[32,16,1024]{2,1,0:T(8,128)(2,1)}), bf16[32,16,1024]{2,1,0:T(8,128)(2,1)S(1)}, u32[]{:S(2)}, u32[]{:S(2)}) async-start(bf16[32,16,1024]{2,1,0:T(8,128)(2,1)} %bitcast.58), calls=%async_computation.1 | async-start | bytes 2097152 | tf_op jit(solution)/shard_map/all_to_all | solution.py:387
  139.1 18.0 %collective-permute-start.16 = (bf16[256,640]{1,0:T(8,128)(2,1)S(1)}, bf16[256,640]{1,0:T(8,128)(2,1)S(1)}, u32[]{:S(2)}, u32[]{:S(2)}) collective-permute-start(bf16[256,640]{1,0:T(8,128)(2,1)S(1)} %dynamic-slice_bitcast_fusion.1), channel_id=1, source_target_pairs={{0,4},{1,5},{2,6},{3,7},{4,0},{5,1},{6,2},{7,3},{8,12},{9,13},{10,... | collective-permute-start | bytes 983048 | tf_op jit(solution)/shard_map/ppermute | solution.py:477
  142.4 15.4 %collective-permute-start.19 = (bf16[256,640]{1,0:T(8,128)(2,1)S(1)}, bf16[256,640]{1,0:T(8,128)(2,1)}, u32[]{:S(2)}, u32[]{:S(2)}) collective-permute-start(bf16[256,640]{1,0:T(8,128)(2,1)S(1)} %broadcast_select_fusion.2), channel_id=1, source_target_pairs={{0,2},{1,3},{2,0},{3,1},{4,6},{5,7},{6,4},{7,5},{8,10},{9,11},{10,... | collective-permute-start | bytes 983048 | tf_op jit(solution)/shard_map/ppermute | solution.py:477
  158.9 10.5 %collective-permute-start.25 = (bf16[128,256]{1,0:T(8,128)(2,1)S(1)}, bf16[128,256]{1,0:T(8,128)(2,1)S(1)}, u32[]{:S(2)}, u32[]{:S(2)}) collective-permute-start(bf16[128,256]{1,0:T(8,128)(2,1)S(1)} %get-tuple-element.131), channel_id=1, source_target_pairs={{0,0},{1,2},{2,8},{3,10},{4,16},{5,18},{6,24},{7,26},{8,4},{9,6},{... | collective-permute-start | bytes 196616 | tf_op jit(solution)/shard_map/ppermute | solution.py:477
  159.6 9.8 %collective-permute-start.26 = (bf16[128,256]{1,0:T(8,128)(2,1)S(1)}, bf16[128,256]{1,0:T(8,128)(2,1)S(1)}, u32[]{:S(2)}, u32[]{:S(2)}) collective-permute-start(bf16[128,256]{1,0:T(8,128)(2,1)S(1)} %get-tuple-element.132), channel_id=1, source_target_pairs={{0,1},{1,3},{2,9},{3,11},{4,17},{5,19},{6,25},{7,27},{8,5},{9,7},{... | collective-permute-start | bytes 196616 | tf_op jit(solution)/shard_map/ppermute | solution.py:477
  163.1 12.3 %collective-permute-start.20 = (bf16[128,1024]{1,0:T(8,128)(2,1)}, bf16[128,1024]{1,0:T(8,128)(2,1)}, u32[]{:S(2)}, u32[]{:S(2)}) collective-permute-start(bf16[128,1024]{1,0:T(8,128)(2,1)} %get-tuple-element.120), channel_id=1, source_target_pairs={{0,0},{1,8},{2,2},{3,10},{4,4},{5,12},{6,6},{7,14},{8,16},{9,24},{... | collective-permute-start | bytes 786440 | tf_op jit(solution)/shard_map/ppermute | solution.py:477
  166.7 14.1 %collective-permute-start.21 = (bf16[128,1024]{1,0:T(8,128)(2,1)S(1)}, bf16[128,1024]{1,0:T(8,128)(2,1)}, u32[]{:S(2)}, u32[]{:S(2)}) collective-permute-start(bf16[128,1024]{1,0:T(8,128)(2,1)S(1)} %get-tuple-element.119), channel_id=1, source_target_pairs={{0,1},{1,9},{2,3},{3,11},{4,5},{5,13},{6,7},{7,15},{8,17},{9,25},{... | collective-permute-start | bytes 786440 | tf_op jit(solution)/shard_map/ppermute | solution.py:477
  (25 other events, 103.8 us)
where the time goes:
time: 184 us; the launch traced here: 183 us
  starting transfers between devices  55.9 us (30%)
  Pallas kernels  46.6 us (25%)
  waiting for transfers between devices  33.6 us (18%)
  matrix products  16.4 us (9%)
  other arithmetic  16.2 us (9%)
  local copies, waits for them, and re-layouts  13.2 us (7%)
    ppermute x27, starting transfers between devices, send(): return lax.ppermute(array, ('seq', 'dp'), steps)  41.6 us
    ppermute x27, waiting for transfers between devices, send(): return lax.ppermute(array, ('seq', 'dp'), steps)  27.3 us
    pallas_call x1, Pallas kernels, forward_attention(): pl.pallas_call(functools.partial(forward_kernel, blk=blk, users=users, ma...  20 us
    pallas_call x1, Pallas kernels, backward_attention(): pl.pallas_call(functools.partial(backward_kernel, blk=blk, users=users, m...  19.1 us
    all_to_all x2, starting transfers between devices, to_owners(): lax.all_to_all(rows.reshape(shape), ('seq', 'dp'), split_axis=0, concat_a...  14.3 us
    dot_general x6, matrix products, dot_nt(): lax.dot_general(a, b, (((1,), (1,)), ((), ())), preferred_element_type=F32)  7.4 us
    all_to_all x2, waiting for transfers between devices, to_owners(): lax.all_to_all(rows.reshape(shape), ('seq', 'dp'), split_axis=0, concat_a...  6.27 us
    unnamed x54, local copies, waits for them, and re-layouts  4.92 us
  transfers between devices with their start and end apart: 29, of which 8 were waited for; matrix products, arithmetic and copies ran while one was open for 18% of the time, Pallas kernels for 24%

commit v1 on v0

--- a/solution.py
+++ b/solution.py
@@ -153,10 +153,12 @@
     order_ref = refs[0]
     mg_refs = refs[1 : 1 + count]
     gate_ref, heads_ref, mg_out_ref, stats_ref = refs[1 + count :]
-    rows = mg_refs[0].shape[0]
-    for b in range(count):
+    blocks = order_ref.shape[0]
+    rows = gate_ref.shape[0] // blocks
+    chunks = blocks // count
+    for b in range(blocks):
         at = pl.ds(pl.multiple_of(order_ref[b] * rows, rows), rows)
-        mg = mg_refs[b][...]
+        mg = mg_refs[b // chunks][b % chunks * rows : (b % chunks + 1) * rows, :]
         mg_out_ref[at, :] = mg
         ng = mg.astype(F32) * gate_ref[at, :]
         heads = heads_ref[at, :].astype(F32)
@@ -312,19 +314,25 @@
     )(lengths, *stats, mg, gate, head_outs, acts, slopes, weights, score_slope)
 
 
-def update_kernel(ids_ref, rows_ref, table_ref, accum_ref, new_table_ref, new_accum_ref):
+def update_kernel(rows_ref, table_ref, accum_ref, new_table_ref, new_accum_ref, ids):
     i = pl.program_id(0)
     blk = table_ref.shape[0]
     slots = rows_ref.shape[0]
+
+    @pl.when(i == 0)
+    def _():
+        numbers = jnp.transpose(rows_ref[:, D:].astype(F32))
+        ids[...] = (numbers[0:1, :] * 256.0 + numbers[1:2, :]).astype(jnp.int32)
+
     row = i * blk + lax.broadcasted_iota(jnp.int32, (blk, slots), 0)
-    hits = jnp.where(row == ids_ref[...], 1.0, 0.0).astype(BF)
-    grad = dot_nn(hits, rows_ref[...])
+    hits = jnp.where(row == ids[...], 1.0, 0.0).astype(BF)
+    grad = dot_nn(hits, rows_ref[:, :D])
     accum = jnp.transpose(jnp.broadcast_to(accum_ref[...], (128, blk)))[:, :1] + jnp.mean(grad * grad, axis=1, keepdims=True)
     new_accum_ref[...] = jnp.transpose(jnp.broadcast_to(accum, (blk, 128)))[:1, :]
     new_table_ref[...] = table_ref[...] - LEARN_RATE * grad * lax.rsqrt(accum)
 
 
-def update_rows(got_ids, got_rows, emb_table, row_accum):
+def update_rows(got_rows, emb_table, row_accum):
     rows_own = emb_table.shape[0]
     slots = got_rows.shape[0]
     blk = min(256, rows_own)
@@ -332,8 +340,7 @@
         update_kernel,
         grid=(rows_own // blk,),
         in_specs=[
-            pl.BlockSpec((1, slots), lambda i: (0, 0)),
-            pl.BlockSpec((slots, D), lambda i: (0, 0)),
+            pl.BlockSpec((slots, D + 128), lambda i: (0, 0)),
             pl.BlockSpec((blk, D), lambda i: (i, 0)),
             pl.BlockSpec((1, blk), lambda i: (0, i)),
         ],
@@ -345,12 +352,13 @@
             jax.ShapeDtypeStruct((rows_own, D), F32),
             jax.ShapeDtypeStruct((1, rows_own), F32),
         ],
+        scratch_shapes=[pltpu.VMEM((1, slots), jnp.int32)],
         compiler_params=pltpu.CompilerParams(vmem_limit_bytes=VMEM_LIMIT),
         cost_estimate=pl.CostEstimate(
             flops=2 * rows_own * slots * D, bytes_accessed=8 * rows_own * D + 2 * slots * D, transcendentals=rows_own
         ),
         name="update_rows",
-    )(got_ids.reshape(1, slots), got_rows, emb_table, row_accum.reshape(1, rows_own))
+    )(got_rows, emb_table, row_accum.reshape(1, rows_own))
     return new_table, new_accum.reshape(rows_own)
 
 
@@ -369,34 +377,29 @@
     return attn, jnp.concatenate([piece[:, 3 * PAIR :] for piece in pieces], axis=1)
 
 
-def row_slots(owners, devices, capacity):
+def row_slots(owners, rows, devices, capacity):
     events = owners.shape[0]
     owner_hits = (owners[:, None] == jnp.arange(devices, dtype=jnp.int32)[None, :]).astype(BF)
     place = jnp.arange(events, dtype=jnp.int32)
     before = (place[:, None] > place[None, :]).astype(BF)
     earlier = jnp.dot(before, owner_hits, preferred_element_type=F32)
-    return owners * capacity + jnp.sum(earlier * owner_hits.astype(F32), axis=1).astype(jnp.int32)
-
-
-def slot_table(flat_slot, slots):
-    return jnp.arange(slots, dtype=jnp.int32)[:, None] == flat_slot[None, :]
+    slots = jnp.sum(earlier * owner_hits.astype(F32), axis=1).astype(jnp.int32)
+    flat_slot = owners * capacity + slots
+    slot_hits = jnp.arange(devices * capacity, dtype=jnp.int32)[:, None] == flat_slot[None, :]
+    lane = jnp.arange(128, dtype=jnp.int32)[None, :]
+    numbers = jnp.where(lane == 0, rows[:, None] // 256, jnp.where(lane == 1, rows[:, None] % 256, 0))
+    return slot_hits.astype(BF), numbers.astype(BF)
+
+
+def rows_by_slot(slot_matrix, input_grad, numbers):
+    rows = jnp.concatenate([input_grad.astype(BF), numbers], axis=1)
+    return jnp.dot(slot_matrix, rows, preferred_element_type=F32).astype(BF)
 
 
 def to_owners(rows, devices, capacity):
     shape = (devices, capacity) + rows.shape[1:]
     got = lax.all_to_all(rows.reshape(shape), ("seq", "dp"), split_axis=0, concat_axis=0, tiled=True)
     return got.reshape(rows.shape)
-
-
-def ids_to_owners(flat_slot, item_row, rows_own, devices, capacity):
-    filled = slot_table(flat_slot, devices * capacity)
-    ids = jnp.min(jnp.where(filled, item_row[None, :], rows_own), axis=1).astype(jnp.int32)
-    return to_owners(ids, devices, capacity)
-
-
-def rows_by_slot(flat_slot, input_grad, slots):
-    filled = slot_table(flat_slot, slots).astype(BF)
-    return jnp.dot(filled, input_grad.astype(BF), preferred_element_type=F32).astype(BF)
 
 
 TN = (((0,), (0,)), ((), ()))
@@ -423,8 +426,7 @@
 
     w_own = own_weights(w_attn, w_gate, seq_id, pairs)
     w_out_own = lax.dynamic_slice_in_dim(w_out, seq_id * cols, cols, 0)
-    flat_slot = row_slots(item_owner[:, 0], devices, capacity)
-    got_ids = ids_to_owners(flat_slot, item_row, emb_table.shape[0], devices, capacity)
+    slot_matrix, numbers = row_slots(item_owner[:, 0], item_row, devices, capacity)
 
     x_full = lax.all_gather(layer_input, "seq", axis=0, tiled=True)
     og_full = lax.all_gather(out_grad, "seq", axis=0, tiled=True)
@@ -444,8 +446,8 @@
         input_part.reshape(seq_count, tokens_dev, D), "seq", split_axis=0, concat_axis=0, tiled=True
     )
     input_grad = jnp.sum(got.astype(F32), axis=0) + out_grad.astype(F32)
-    got_rows = to_owners(rows_by_slot(flat_slot, input_grad, devices * capacity), devices, capacity)
-    new_table, new_accum = update_rows(got_ids, got_rows, emb_table, row_accum)
+    got_rows = to_owners(rows_by_slot(slot_matrix, input_grad, numbers), devices, capacity)
+    new_table, new_accum = update_rows(got_rows, emb_table, row_accum)
 
     out_part = dot_tn(mixed, og_full).astype(BF)
     share = dp_count // seq_count
@@ -483,6 +485,14 @@
 
 def swap_far(array):
     return send(array, lambda s, e, c: None if home(s, c) else (3 - s, e, 1 - c))
+
+
+def swap_near_home(array):
+    return send(array, lambda s, e, c: (s ^ 1, e, c) if home(s, c) else None)
+
+
+def swap_near_far(array):
+    return send(array, lambda s, e, c: None if home(s, c) else (s ^ 1, e, c))
 
 
 def fetch_near(array):
@@ -544,28 +554,36 @@
     x_far = swap_far(layer_input)
     x_near = fetch_near(layer_input)
     users = lengths.shape[1]
-    flat_slot = row_slots(item_owner[:, 0], devices, capacity)
-    small = jnp.concatenate([flat_slot[None, :], jnp.pad(lengths, ((0, 0), (0, 128 - users)))], axis=1)
+    keys = (item_owner[:, 0] * rows_own + item_row).reshape(1, tokens_dev)
+    small = jnp.concatenate([keys, jnp.pad(lengths, ((0, 0), (0, 128 - users)))], axis=1)
     small = jnp.where(at_home, small, swap_far(small))
-    lengths = small[:, tokens_dev : tokens_dev + users]
-    got_ids = ids_to_owners(flat_slot, item_row, rows_own, devices, capacity)
+    keys, lengths = small[0, :tokens_dev], small[:, tokens_dev : tokens_dev + users]
     w_own = own_weights(w_attn, w_gate, part, pairs)
+    slot_matrix, numbers = row_slots(keys // rows_own, keys % rows_own, devices, capacity)
     mg_own = dot_nt(out_grad, w_out).astype(BF)
-    mg_sent = [lax.dynamic_slice_in_dim(mg_own, (s + k) % SEQ * cols, cols, 1) for k in range(SEQ)]
-    x_far, x_near, w_own, lengths, got_ids, *mg_sent = tie(x_far, x_near, w_own, lengths, got_ids, *mg_sent)
+    x_far, x_near, w_own, slot_matrix, numbers, lengths, mg_own = tie(
+        x_far, x_near, w_own, slot_matrix, numbers, lengths, mg_own
+    )
     x_here = jnp.concatenate([jnp.where(at_home, layer_input, x_far), x_near], axis=0)
     x_there = swap_core(x_here)
-    x_here, *mg_sent = tie(x_here, *mg_sent)
-    mg_blocks = []
-    for k, piece in enumerate(mg_sent):
-        mg_blocks.append(send(piece, lambda s, e, c: (2 * c + (s + k) % SEQ // 2, e, (s + k) % SEQ % 2)))
-    mg_order = jnp.stack([(part - k) % SEQ for k in range(SEQ)]).astype(jnp.int32)
+
+    x_here, mg_own = tie(x_here, mg_own)
+    mg_even, mg_odd = mg_own[:, : D // 2], mg_own[:, D // 2 :]
+    even = s % 2 == 0
+    mg_kept, mg_sent = jnp.where(even, mg_even, mg_odd), jnp.where(even, mg_odd, mg_even)
+    mg_first = send(mg_sent, lambda s, e, c: (s ^ 1, e, c) if home(s, c) else (3 - s, e, 1 - c))
+    mg_second = send(mg_kept, lambda s, e, c: None if home(s, c) else ((3 - s) ^ 1, e, 1 - c))
 
     x_full, acts, slopes, gate, weights, score_slope, heads = forward_attention(
         lengths, order, [x_here, x_there], w_own, blk, maxlen
     )
-    heads, *mg_blocks = tie(heads, *mg_blocks)
-    mg, stats_own = event_stats(mg_order, mg_blocks, gate, heads)
+    heads, mg_first, mg_second = tie(heads, mg_first, mg_second)
+    mg_mine = jnp.where(at_home, mg_kept, mg_first)
+    mg_near = jnp.where(at_home, mg_first, mg_second)
+    mg_both = jnp.concatenate([mg_mine, mg_near], axis=0)
+    mg_here = jnp.where(c == 0, mg_both[:, :cols], mg_both[:, cols:])
+    mg_there = swap_core(jnp.where(c == 0, mg_both[:, cols:], mg_both[:, :cols]))
+    mg, stats_own = event_stats(order, [mg_here, mg_there], gate, heads)
     stats = [
         stats_own,
         swap_core(stats_own),
@@ -574,65 +592,62 @@
     ]
     *stats, og_own = tie(*stats, out_grad)
     og_far = swap_far(og_own)
-    og_near = fetch_near(og_own)
+    og_near_home = swap_near_home(og_own)
     grads, mixed = backward_attention(
         lengths, stats, mg, gate, heads, acts, slopes, weights, score_slope, blk, maxlen
     )
 
-    def input_part(grads, block, columns=slice(None)):
-        return dot_nt(lax.dynamic_slice_in_dim(grads, block * tokens_dev, tokens_dev, 0), w_own[columns])
-
-    og_far, og_near, grads = tie(og_far, og_near, grads)
-    from_diag, near_sums, from_near = [], [], []
-    column_halves = (slice(0, D // 2), slice(D // 2, D))
-    for columns in column_halves:
-        from_diag.append(swap_core(input_part(grads, diag_at, columns).astype(BF)))
-    for columns, got in zip(column_halves, from_diag):
-        near_sums.append((input_part(grads, near_at, columns) + got.astype(F32)).astype(BF))
-        from_near.append(swap_near(near_sums[-1]))
-    *near_sums, grads, og_far, og_near = tie(*near_sums, grads, og_far, og_near)
-    core_part = input_part(grads, core_at).astype(BF)
-    from_core = swap_core(core_part)
-    og_mine = jnp.where(at_home, out_grad, og_far)
-    input_grad = input_part(grads, mine_at) + og_mine.astype(F32)
-
-    core_part, grads, mixed = tie(core_part, grads, mixed)
-    half = 5 * cols // 2
-    rest = 4 * cols - half
+    grads, og_far, og_near_home = tie(grads, og_far, og_near_home)
+
+    def input_part(grads, block):
+        return dot_nt(lax.dynamic_slice_in_dim(grads, block * tokens_dev, tokens_dev, 0), w_own)
+
+    diag_part = input_part(grads, diag_at).astype(BF)
+    from_diag = swap_core(diag_part)
+    diag_part, grads = tie(diag_part, grads)
+    near_part = input_part(grads, near_at)
+    near_part, from_diag = tie(near_part, from_diag)
+    near_sum = (near_part + from_diag.astype(F32)).astype(BF)
+    from_near = swap_near(near_sum)
+    near_sum, grads = tie(near_sum, grads)
+    half = 2 * cols
     proj = dot_tn(x_full, grads).astype(BF).reshape(2, 2, D // PLANE, 4 * cols)
     a_kept, a_sent = halves(proj[..., :half], x, 1)
     b_kept, b_sent = halves(proj[..., half:], y, 0)
+    a_sent, b_sent, grads = tie(a_sent, b_sent, grads)
     a_got = swap_x(a_sent)
+    b_got = swap_y(b_sent)
+    core_part = input_part(grads, core_at).astype(BF)
+    from_core = swap_core(core_part)
+    mine_part = input_part(grads, mine_at)
+    og_mine = jnp.where(at_home, out_grad, og_far)
+    input_grad = mine_part + from_core.astype(F32) + from_near.astype(F32) + og_mine.astype(F32)
+    rows = rows_by_slot(slot_matrix, input_grad, numbers)
+    rows, a_got, b_got, og_mine, og_near_home, mixed = tie(rows, a_got, b_got, og_mine, og_near_home, mixed)
+    got_rows = to_owners(rows, devices, capacity)
+    a = (a_kept.astype(F32) + a_got.astype(F32)).astype(BF)
+    a_kept, a_sent = halves(a, y, 0)
+    b = (b_kept.astype(F32) + b_got.astype(F32)).astype(BF)
+    b_kept, b_sent = halves(b, x, 0)
+    a_sent, b_sent, og_mine = tie(a_sent, b_sent, og_mine)
+    a_got = swap_y(a_sent)
+    b_got = swap_x(b_sent)
+    og_near = jnp.where(at_home, og_near_home, swap_near_far(og_mine))
+
+    def picked(bit, low, high):
+        return jnp.where(bit == 0, low, high)
+
     og_here = jnp.concatenate([og_mine, og_near], axis=0)
     og_there = swap_core(og_here)
-    a_sent, mixed = tie(a_sent, mixed)
     mixed_rows = [lax.dynamic_slice_in_dim(mixed, at * tokens_dev, tokens_dev, 0) for at in (mine_at, near_at, core_at, diag_at)]
     out_part = dot_tn(jnp.concatenate(mixed_rows[:2], axis=0), og_here)
     out_part = (out_part + dot_tn(jnp.concatenate(mixed_rows[2:], axis=0), og_there)).astype(BF)
-
-    def picked(bit, low, high):
-        return jnp.where(bit == 0, low, high)
-
-    def b_message(rows, out):
-        return jnp.concatenate([rows[0], rows[1], out], axis=1)
-
     low, high = out_part[:, : D // 2], out_part[:, D // 2 :]
-    b_kept = b_message(b_kept, picked(y, low, high))
-    b_sent = b_message(b_sent, picked(y, high, low))
-    b_got = swap_y(b_sent)
-
-    input_grad = input_grad + from_core.astype(F32) + jnp.concatenate(from_near, axis=1).astype(F32)
-    got_rows = to_owners(rows_by_slot(small[0, :tokens_dev], input_grad, devices * capacity), devices, capacity)
+    out = picked(y, low, high).astype(F32) + swap_y(picked(y, high, low)).astype(F32)
+    out = out.astype(BF)
 
     a = (a_kept.astype(F32) + a_got.astype(F32)).astype(BF)
-    a_kept, a_sent = halves(a, y, 0)
-    a_got = swap_y(a_sent)
     b = (b_kept.astype(F32) + b_got.astype(F32)).astype(BF)
-    b0 = jnp.concatenate([b[:, :rest], b[:, 2 * rest : 2 * rest + cols]], axis=1)
-    b1 = jnp.concatenate([b[:, rest : 2 * rest], b[:, 2 * rest + cols :]], axis=1)
-    b_got = swap_x(picked(x, b1, b0))
-    a = (a_kept.astype(F32) + a_got.astype(F32)).astype(BF)
-    b = (picked(x, b0, b1).astype(F32) + b_got.astype(F32)).astype(BF)
 
     def last(array, target):
         pieces = array.reshape(2, D // (2 * PLANE), array.shape[1])
@@ -640,13 +655,13 @@
         one = send(one, lambda s, e, c: target(s, e, c, s // 2))
         return one, send(other, lambda s, e, c: target(s, e, c, 1 - s // 2))
 
-    proj = last(jnp.concatenate([a, b[:, :rest]], axis=1), lambda s, e, c, piece: (2 * (s % 2) + c, e, piece))
-    out = last(b[:, rest:], lambda s, e, c, piece: (e, 2 * (s % 2) + c, piece))
-    ids = got_ids.reshape(SEQ, PLANE, 2, capacity)
-    at_seq = jnp.arange(SEQ, dtype=jnp.int32)[:, None, None, None]
-    at_core = jnp.arange(2, dtype=jnp.int32)[None, None, :, None]
-    ids = jnp.where(at_core == at_seq // 2, ids, ids[::-1, :, ::-1])
-    new_table, new_accum = update_rows(ids, got_rows, emb_table, row_accum)
+    proj = jnp.concatenate([a, b], axis=1)
+    low, high = out[:, :cols], out[:, cols:]
+    out = picked(x, low, high).astype(F32) + swap_x(picked(x, high, low)).astype(F32)
+    proj, out, row_accum = tie(proj, out.astype(BF), row_accum)
+    proj = last(proj, lambda s, e, c, piece: (2 * (s % 2) + c, e, piece))
+    out = last(out, lambda s, e, c, piece: (e, 2 * (s % 2) + c, piece))
+    new_table, new_accum = update_rows(got_rows, emb_table, row_accum)
     *proj, new_accum = tie(*proj, new_accum)
     grad_attn, grad_gate = attn_and_gate(proj[0].astype(F32) + proj[1].astype(F32), pairs)
     return (grad_attn, grad_gate, out[0].astype(F32) + out[1].astype(F32), new_table, new_accum)

time: 184 us -> 193 us (1.049)
  starting transfers between devices: 55.9 us -> 65.5 us
  waiting for transfers between devices: 33.6 us -> 39 us
  Pallas kernels: 46.6 us -> 43 us
  local copies, waits for them, and re-layouts: 13.2 us -> 10.1 us
    ppermute x27, starting transfers between devices: 41.6 us -> 61.8 us  [send(): return lax.ppermute(array, ('seq', 'dp'), steps)]
    ppermute x27, waiting for transfers between devices: 27.3 us -> 39 us  [send(): return lax.ppermute(array, ('seq', 'dp'), steps)]
    all_to_all x2 -> x1, starting transfers between devices: 14.3 us -> 3.69 us  [to_owners(): lax.all_to_all(rows.reshape(shape), ('seq', 'dp'), split_axis=0, concat_a...]
    all_to_all x2 -> x1, waiting for transfers between devices: 6.27 us -> 0.01 us  [to_owners(): lax.all_to_all(rows.reshape(shape), ('seq', 'dp'), split_axis=0, concat_a...]
    dot_general x6 -> x5, matrix products: 7.4 us -> 10.3 us  [dot_nt(): lax.dot_general(a, b, (((1,), (1,)), ((), ())), preferred_element_type=F32)]
    dot_general x1, matrix products: 3.7 us -> 1.53 us  [rows_by_slot(): return jnp.dot(slot_matrix, rows, preferred_element_type=F32).astype(BF)]
    unnamed x54 -> x48, local copies, waits for them, and re-layouts: 4.92 us -> 3.48 us
  transfers between devices with their start and end apart: 29 -> 28, of which waited for: 8 -> 11; matrix products, arithmetic and copies ran while one was open for 18% -> 15% of each run, Pallas kernels for 24% -> 21%
where the time goes in v1:
time: 193 us; the launch traced here: 191 us
  starting transfers between devices  65.5 us (34%)
  Pallas kernels  43 us (22%)
  waiting for transfers between devices  39 us (20%)
  matrix products  16.7 us (9%)
  other arithmetic  15.3 us (8%)
  local copies, waits for them, and re-layouts  10.1 us (5%)
    ppermute x27, starting transfers between devices, send(): return lax.ppermute(array, ('seq', 'dp'), steps)  61.8 us
    ppermute x27, waiting for transfers between devices, send(): return lax.ppermute(array, ('seq', 'dp'), steps)  39 us
    pallas_call x1, Pallas kernels, forward_attention(): pl.pallas_call(functools.partial(forward_kernel, blk=blk, users=users, ma...  18.3 us
    pallas_call x1, Pallas kernels, backward_attention(): pl.pallas_call(functools.partial(backward_kernel, blk=blk, users=users, m...  17.3 us
    dot_general x5, matrix products, dot_nt(): lax.dot_general(a, b, (((1,), (1,)), ((), ())), preferred_element_type=F32)  10.3 us
    dot_general x3, matrix products, dot_tn(): return lax.dot_general(a, b, TN, preferred_element_type=F32)  4.66 us
    pallas_call x1, Pallas kernels, update_rows(): pl.pallas_call(update_kernel, grid=(rows_own // blk,), in_specs=[pl.Block...  4.34 us
  transfers between devices with their start and end apart: 28, of which 11 were waited for; matrix products, arithmetic and copies ran while one was open for 15% of the time, Pallas kernels for 21%

profile of v1, /device:TPU:0, one launch (start us, length us, event | category | flops | bytes accessed | tf_op | source)
XLA Modules:
  0.0 190.9 jit_solution(11991899127799816214)
XLA Ops:
  1.5 3.1 %collective-permute-start.1 = (bf16[256,1024]{1,0:T(8,128)(2,1)}, bf16[256,1024]{1,0:T(8,128)(2,1)}, u32[]{:S(2)}, u32[]{:S(2)}) collective-permute-start(bf16[256,1024]{1,0:T(8,128)(2,1)} %param.10), channel_id=1, source_target_pairs={{0,8},{1,16},{2,10},{3,18},{4,12},{5,20},{6,14},{7,22},{8,0},{9,24... | collective-permute-start | bytes 1572872 | tf_op jit(solution)/shard_map/ppermute | solution.py:479
  7.3 1.8 convolution_convert_fusion.4
  10.2 1.5 constant_dynamic-slice_fusion.7
  11.8 1.6 pad_maximum_fusion.refs_4_
  15.7 16.4 %collective-permute-start.3 = (bf16[512,1024]{1,0:T(8,128)(2,1)S(1)}, bf16[512,1024]{1,0:T(8,128)(2,1)S(1)}, u32[]{:S(2)}, u32[]{:S(2)}) collective-permute-start(bf16[512,1024]{1,0:T(8,128)(2,1)S(1)} %pad_maximum_fusion.1.refs_2_), channel_id=1, source_target_pairs={{0,1},{1,0},{2,3},{3,2},{4,5},{5,4},{6,7},{7,6},{8,9},{9,8},{10,11... | collective-permute-start | bytes 3145736 | tf_op jit(solution)/shard_map/ppermute | solution.py:479
  32.8 1.6 collective-permute-start.4
  36.1 18.3 %attention_forward.1 = (bf16[1024,1024]{1,0:T(8,128)(2,1)}, bf16[1024,1024]{1,0:T(8,128)(2,1)}, bf16[1024,1024]{1,0:T(8,128)(2,1)}, f32[1024,256]{1,0:T(8,128)},...) custom-call(s32[1,3]{1,0:T(1,128)} %slice.73.refs_0_, ...), custom_call_target="tpu_custom_call" | custom-call | flops 4294967296 | bytes 12582912 | tf_op jit(solution)/shard_map/attention_forward/pallas_call | solution.py:134
  55.2 2.6 %collective-permute-start.6 = (bf16[512,256]{1,0:T(8,128)(2,1)S(1)}, bf16[512,256]{1,0:T(8,128)(2,1)S(1)}, u32[]{:S(2)}, u32[]{:S(2)}) collective-permute-start(bf16[512,256]{1,0:T(8,128)(2,1)S(1)} %get-tuple-element.133), channel_id=1, source_target_pairs={{0,1},{1,0},{2,3},{3,2},{4,5},{5,4},{6,7},{7,6},{8,9},{9,8},{10,11... | collective-permute-start | bytes 786440 | tf_op jit(solution)/shard_map/ppermute | solution.py:479
  59.7 3.1 %event_stats.1 = (bf16[1024,256]{1,0:T(8,128)(2,1)}, f32[8,1024]{1,0:T(8,128)}) custom-call(s32[4]{0:T(128)} %pad_add_fusion.1.refs_1_.refs_0_, bf16[512,256]{1,0:T(8,128)(2,1)} %get-tuple-element.134.refs_1_, bf16[512,256]{1,0:T(8,128)(2,1)} %copy-done.16, f32[1024,256]{1,0:T(8,128)} %get-tuple-element.71.refs_3_.refs_6_, ...), custom_call_target="tpu_custom_call" | custom-call | flops 5242880 | bytes 2621440 | tf_op jit(solution)/shard_map/event_stats/pallas_call | solution.py:179
  64.7 2.6 %collective-permute-done.8.refs_3_ = f32[8,1024]{1,0:T(8,128)S(1)} collective-permute-done((f32[8,1024]{1,0:T(8,128)}, f32[8,1024]{1,0:T(8,128)S(1)}, u32[]{:S(2)}, u32[]{:S(2)}) %collective-permute-start.8) | collective-permute-done | bytes 32800 | tf_op jit(solution)/shard_map/ppermute | solution.py:479
  70.5 2.8 %collective-permute-start.11 = (bf16[256,1024]{1,0:T(8,128)(2,1)S(1)}, bf16[256,1024]{1,0:T(8,128)(2,1)S(1)}, u32[]{:S(2)}, u32[]{:S(2)}) collective-permute-start(bf16[256,1024]{1,0:T(8,128)(2,1)S(1)} %copy-done.12), channel_id=1, source_target_pairs={{0,8},{2,10},{4,12},{6,14},{8,0},{10,2},{12,4},{14,6},{17,25},{19,... | collective-permute-start | bytes 1572872 | tf_op jit(solution)/shard_map/ppermute | solution.py:479
  73.3 17.3 %attention_backward.1 = (bf16[1024,1024]{1,0:T(8,128)(2,1)}, bf16[1024,256]{1,0:T(8,128)(2,1)}) custom-call(s32[1,3]{1,0:T(1,128)} %slice.73.refs_0_, f32[8,1024]{1,0:T(8,128)} %get-tuple-element.74.refs_1_, f32[8,1024]{1,0:T(8,128)} %copy-done.18, f32[8,1024]{1,0:T(8,128)} %copy-done.19, f32[8,1024]{1,0:T(8,128)} %copy-done.20, ...), custom_call_target="tpu_custom_call" | custom-call | flops 4294967296 | bytes 15204352 | tf_op jit(solution)/shard_map/attention_backward/pallas_call | solution.py:282
  90.6 2.8 %convolution_convert_fusion.3 = bf16[256,1024]{1,0:T(8,128)(2,1)} fusion(bf16[1024,1024]{1,0:T(8,128)(2,1)S(1)} %copy-done.2, bf16[1024,1024]{1,0:T(8,128)(2,1)} %get-tuple-element.91, s32[]{:T(128)S(6)} %select_n.270), kind=kOutput, calls=%fused_computation.9 | convolution fusion | flops 537133056 | bytes 3145732 | tf_op jit(solution)/shard_map/dot_general | solution.py:27
  94.5 1.9 %fusion.14 = f32[256,1024]{1,0:T(8,128)S(1)} fusion(bf16[1024,1024]{1,0:T(8,128)(2,1)S(1)} %copy-done.2, bf16[1024,1024]{1,0:T(8,128)(2,1)} %get-tuple-element.91, s32[]{:T(128)S(6)} %select_n.271), kind=kOutput, calls=%fused_computation.37 | convolution fusion | flops 536870912 | bytes 3670020 | tf_op jit(solution)/shard_map/dot_general | solution.py:27
  97.8 2.4 %convolution_convert_fusion.1 = bf16[1024,1024]{1,0:T(8,128)(2,1)S(1)} fusion(bf16[1024,1024]{1,0:T(8,128)(2,1)S(1)} %copy-done.23, bf16[1024,1024]{1,0:T(8,128)(2,1)S(1)} %copy-done.17), kind=kOutput, calls=%fused_computation.2 | convolution fusion | flops 2148532224 | bytes 6291456 | tf_op jit(solution)/shard_map/dot_general | solution.py:409
  102.2 1.5 convolution_convert_fusion.2
  104.9 1.6 collective-permute-start.15
  106.5 5.1 %collective-permute-start.16 = (bf16[2,256,512]{2,1,0:T(8,128)(2,1)}, bf16[2,256,512]{2,1,0:T(8,128)(2,1)S(1)}, u32[]{:S(2)}, u32[]{:S(2)}) collective-permute-start(bf16[2,256,512]{2,1,0:T(8,128)(2,1)} %dynamic-slice_bitcast_fusion), channel_id=1, source_target_pairs={{0,4},{1,5},{2,6},{3,7},{4,0},{5,1},{6,2},{7,3},{8,12},{9,13},{10,... | collective-permute-start | bytes 1572872 | tf_op jit(solution)/shard_map/ppermute | solution.py:479
  111.8 2.2 %fusion.3 = bf16[256,1024]{1,0:T(8,128)(2,1)S(1)} fusion(bf16[1024,1024]{1,0:T(8,128)(2,1)S(1)} %copy-done.2, bf16[256,1024]{1,0:T(8,128)(2,1)S(1)} %broadcast_select_fusion.1, bf16[256,1024]{1,0:T(8,128)(2,1)} %collective-permute-done.14, bf16[256,1024]{1,0:T(8,128)(2,1)} %collective-permute-done.13, bf16[1024,1024]{1,0:T(8,128)(2,1)} %get-tuple-element.91, ...), kind=kOutput, calls=%fused_computation.11 | convolution fusion | flops 538705920 | bytes 4718596 | tf_op jit(solution)/shard_map/dot_general | solution.py:27
  114.0 1.5 convolution_convert_fusion
  115.6 3.9 %collective-permute-done.15 = bf16[2,256,512]{2,1,0:T(8,128)(2,1)S(1)} collective-permute-done((bf16[2,256,512]{2,1,0:T(8,128)(2,1)}, bf16[2,256,512]{2,1,0:T(8,128)(2,1)S(1)}, u32[]{:S(2)}, u32[]{:S(2)}) %collective-permute-start.15) | collective-permute-done | bytes 524320 | tf_op jit(solution)/shard_map/ppermute | solution.py:479
  119.5 4.6 %collective-permute-done.16 = bf16[2,256,512]{2,1,0:T(8,128)(2,1)S(1)} collective-permute-done((bf16[2,256,512]{2,1,0:T(8,128)(2,1)}, bf16[2,256,512]{2,1,0:T(8,128)(2,1)S(1)}, u32[]{:S(2)}, u32[]{:S(2)}) %collective-permute-start.16) | collective-permute-done | bytes 524320 | tf_op jit(solution)/shard_map/ppermute | solution.py:479
  127.1 8.8 %collective-permute-start.20 = (bf16[512,1024]{1,0:T(8,128)(2,1)}, bf16[512,1024]{1,0:T(8,128)(2,1)}, u32[]{:S(2)}, u32[]{:S(2)}) collective-permute-start(bf16[512,1024]{1,0:T(8,128)(2,1)} %pad_maximum_fusion.2), channel_id=1, source_target_pairs={{0,1},{1,0},{2,3},{3,2},{4,5},{5,4},{6,7},{7,6},{8,9},{9,8},{10,11... | collective-permute-start | bytes 3145736 | tf_op jit(solution)/shard_map/ppermute | solution.py:479
  136.5 3.7 %all-to-all-start = ((bf16[32,16,1152]{2,1,0:T(8,128)(2,1)}), bf16[32,16,1152]{2,1,0:T(8,128)(2,1)S(1)}, u32[]{:S(2)}, u32[]{:S(2)}) async-start(bf16[32,16,1152]{2,1,0:T(8,128)(2,1)} %bitcast.21), calls=%async_computation | async-start | bytes 2359296 | tf_op jit(solution)/shard_map/all_to_all | solution.py:401
  140.3 1.8 fusion.22
  143.2 1.6 collective-permute-start.21
  146.6 13.2 %collective-permute-done.21 = bf16[256,512]{1,0:T(8,128)(2,1)S(1)} collective-permute-done((bf16[256,512]{1,0:T(8,128)(2,1)}, bf16[256,512]{1,0:T(8,128)(2,1)S(1)}, u32[]{:S(2)}, u32[]{:S(2)}) %collective-permute-start.21) | collective-permute-done | bytes 262176 | tf_op jit(solution)/shard_map/ppermute | solution.py:479
  161.4 5.4 %collective-permute-done.17 = bf16[256,512]{1,0:T(8,128)(2,1)S(1)} collective-permute-done((bf16[256,512]{1,0:T(8,128)(2,1)S(1)}, bf16[256,512]{1,0:T(8,128)(2,1)S(1)}, u32[]{:S(2)}, u32[]{:S(2)}) %collective-permute-start.17) | collective-permute-done | bytes 262176 | tf_op jit(solution)/shard_map/ppermute | solution.py:479
  168.5 3.6 %collective-permute-start.23 = (bf16[128,1024]{1,0:T(8,128)(2,1)}, bf16[128,1024]{1,0:T(8,128)(2,1)}, u32[]{:S(2)}, u32[]{:S(2)}) collective-permute-start(bf16[128,1024]{1,0:T(8,128)(2,1)} %get-tuple-element.128), channel_id=1, source_target_pairs={{0,0},{1,8},{2,2},{3,10},{4,4},{5,12},{6,6},{7,14},{8,16},{9,24},{... | collective-permute-start | bytes 786440 | tf_op jit(solution)/shard_map/ppermute | solution.py:479
  172.1 3.8 %collective-permute-start.24 = (bf16[128,1024]{1,0:T(8,128)(2,1)S(1)}, bf16[128,1024]{1,0:T(8,128)(2,1)}, u32[]{:S(2)}, u32[]{:S(2)}) collective-permute-start(bf16[128,1024]{1,0:T(8,128)(2,1)S(1)} %get-tuple-element.127), channel_id=1, source_target_pairs={{0,1},{1,9},{2,3},{3,11},{4,5},{5,13},{6,7},{7,15},{8,17},{9,25},{... | collective-permute-start | bytes 786440 | tf_op jit(solution)/shard_map/ppermute | solution.py:479
  177.6 4.3 %update_rows.1 = (f32[512,1024]{1,0:T(8,128)}, f32[1,512]{1,0:T(1,128)}) custom-call(bf16[512,1152]{1,0:T(8,128)(2,1)} %bitcast.58, f32[512,1024]{1,0:T(8,128)} %table_ref.1, f32[1,512]{1,0:T(1,128)} %bitcast.68), custom_call_target="tpu_custom_call" | custom-call | flops 536870912 | bytes 5242880 | tf_op jit(solution)/shard_map/update_rows/pallas_call | solution.py:339
  181.9 6.4 %collective-permute-done.24 = bf16[128,1024]{1,0:T(8,128)(2,1)} collective-permute-done((bf16[128,1024]{1,0:T(8,128)(2,1)S(1)}, bf16[128,1024]{1,0:T(8,128)(2,1)}, u32[]{:S(2)}, u32[]{:S(2)}) %collective-permute-start.24) | collective-permute-done | bytes 262176 | tf_op jit(solution)/shard_map/ppermute | solution.py:479
  (135 shorter events, 36.7 us)
Async XLA Ops:
  0.6 13.8 %collective-permute-start = (bf16[256,1024]{1,0:T(8,128)(2,1)}, bf16[256,1024]{1,0:T(8,128)(2,1)S(1)}, u32[]{:S(2)}, u32[]{:S(2)}) collective-permute-start(bf16[256,1024]{1,0:T(8,128)(2,1)} %param.10), channel_id=1, source_target_pairs={{1,24},{3,26},{5,28},{7,30},{9,16},{11,18},{13,20},{15,22},{16,9},... | collective-permute-start | bytes 1572872 | tf_op jit(solution)/shard_map/ppermute | solution.py:479
  1.5 13.1 %collective-permute-start.1 = (bf16[256,1024]{1,0:T(8,128)(2,1)}, bf16[256,1024]{1,0:T(8,128)(2,1)}, u32[]{:S(2)}, u32[]{:S(2)}) collective-permute-start(bf16[256,1024]{1,0:T(8,128)(2,1)} %param.10), channel_id=1, source_target_pairs={{0,8},{1,16},{2,10},{3,18},{4,12},{5,20},{6,14},{7,22},{8,0},{9,24... | collective-permute-start | bytes 1572872 | tf_op jit(solution)/shard_map/ppermute | solution.py:479
  6.6 6.8 %collective-permute-start.2 = (s32[1,384]{1,0:T(1,128)S(1)}, s32[1,384]{1,0:T(1,128)S(1)}, u32[]{:S(2)}, u32[]{:S(2)}) collective-permute-start(s32[1,384]{1,0:T(1,128)S(1)} %pad_add_fusion), channel_id=1, source_target_pairs={{1,24},{3,26},{5,28},{7,30},{9,16},{11,18},{13,20},{15,22},{16,9},... | collective-permute-start | bytes 4616 | tf_op jit(solution)/shard_map/ppermute | solution.py:479
  15.7 19.3 %copy-start.10 = (bf16[512,1024]{1,0:T(8,128)(2,1)}, bf16[512,1024]{1,0:T(8,128)(2,1)S(1)}, u32[]{:S(2)}) copy-start(bf16[512,1024]{1,0:T(8,128)(2,1)S(1)} %pad_maximum_fusion.1.refs_2_) | copy-start | bytes 3145732
  15.7 19.3 %collective-permute-start.3 = (bf16[512,1024]{1,0:T(8,128)(2,1)S(1)}, bf16[512,1024]{1,0:T(8,128)(2,1)S(1)}, u32[]{:S(2)}, u32[]{:S(2)}) collective-permute-start(bf16[512,1024]{1,0:T(8,128)(2,1)S(1)} %pad_maximum_fusion.1.refs_2_), channel_id=1, source_target_pairs={{0,1},{1,0},{2,3},{3,2},{4,5},{5,4},{6,7},{7,6},{8,9},{9,8},{10,11... | collective-permute-start | bytes 3145736 | tf_op jit(solution)/shard_map/ppermute | solution.py:479
  32.8 21.6 %collective-permute-start.4 = (bf16[256,512]{1,0:T(8,128)(2,1)S(1)}, bf16[256,512]{1,0:T(8,128)(2,1)S(1)}, u32[]{:S(2)}, u32[]{:S(2)}) collective-permute-start(bf16[256,512]{1,0:T(8,128)(2,1)S(1)} %get-tuple-element.136), channel_id=1, source_target_pairs={{0,8},{1,24},{2,10},{3,26},{4,12},{5,28},{6,14},{7,30},{8,0},{9,16... | collective-permute-start | bytes 786440 | tf_op jit(solution)/shard_map/ppermute | solution.py:479
  34.4 20.0 %collective-permute-start.5 = (bf16[256,512]{1,0:T(8,128)(2,1)S(1)}, bf16[256,512]{1,0:T(8,128)(2,1)S(1)}, u32[]{:S(2)}, u32[]{:S(2)}) collective-permute-start(bf16[256,512]{1,0:T(8,128)(2,1)S(1)} %get-tuple-element.135), channel_id=1, source_target_pairs={{1,16},{3,18},{5,20},{7,22},{9,24},{11,26},{13,28},{15,30},{16,1},... | collective-permute-start | bytes 786440 | tf_op jit(solution)/shard_map/ppermute | solution.py:479
  54.4 14.7 %copy-start.12 = (bf16[256,1024]{1,0:T(8,128)(2,1)S(1)}, bf16[256,1024]{1,0:T(8,128)(2,1)}, u32[]{:S(2)}) copy-start(bf16[256,1024]{1,0:T(8,128)(2,1)} %param.11) | copy-start | bytes 1572868
  55.2 3.8 %collective-permute-start.6 = (bf16[512,256]{1,0:T(8,128)(2,1)S(1)}, bf16[512,256]{1,0:T(8,128)(2,1)S(1)}, u32[]{:S(2)}, u32[]{:S(2)}) collective-permute-start(bf16[512,256]{1,0:T(8,128)(2,1)S(1)} %get-tuple-element.133), channel_id=1, source_target_pairs={{0,1},{1,0},{2,3},{3,2},{4,5},{5,4},{6,7},{7,6},{8,9},{9,8},{10,11... | collective-permute-start | bytes 786440 | tf_op jit(solution)/shard_map/ppermute | solution.py:479
  62.8 1.9 collective-permute-start.7
  63.2 4.1 %collective-permute-start.8 = (f32[8,1024]{1,0:T(8,128)}, f32[8,1024]{1,0:T(8,128)S(1)}, u32[]{:S(2)}, u32[]{:S(2)}) collective-permute-start(f32[8,1024]{1,0:T(8,128)} %get-tuple-element.74.refs_1_), channel_id=1, source_target_pairs={{0,8},{1,9},{2,10},{3,11},{4,12},{5,13},{6,14},{7,15},{8,0},{9,1},... | collective-permute-start | bytes 98312 | tf_op jit(solution)/shard_map/ppermute | solution.py:479
  64.6 3.9 %collective-permute-start.9 = (f32[8,1024]{1,0:T(8,128)}, f32[8,1024]{1,0:T(8,128)S(1)}, u32[]{:S(2)}, u32[]{:S(2)}) collective-permute-start(f32[8,1024]{1,0:T(8,128)} %get-tuple-element.74.refs_1_), channel_id=1, source_target_pairs={{0,9},{1,8},{2,11},{3,10},{4,13},{5,12},{6,15},{7,14},{8,1},{9,0},... | collective-permute-start | bytes 98312 | tf_op jit(solution)/shard_map/ppermute | solution.py:479
  69.0 21.6 %collective-permute-start.10 = (bf16[256,1024]{1,0:T(8,128)(2,1)S(1)}, bf16[256,1024]{1,0:T(8,128)(2,1)}, u32[]{:S(2)}, u32[]{:S(2)}) collective-permute-start(bf16[256,1024]{1,0:T(8,128)(2,1)S(1)} %copy-done.12), channel_id=1, source_target_pairs={{1,24},{3,26},{5,28},{7,30},{9,16},{11,18},{13,20},{15,22},{16,9},... | collective-permute-start | bytes 1572872 | tf_op jit(solution)/shard_map/ppermute | solution.py:479
  70.5 20.1 %collective-permute-start.11 = (bf16[256,1024]{1,0:T(8,128)(2,1)S(1)}, bf16[256,1024]{1,0:T(8,128)(2,1)S(1)}, u32[]{:S(2)}, u32[]{:S(2)}) collective-permute-start(bf16[256,1024]{1,0:T(8,128)(2,1)S(1)} %copy-done.12), channel_id=1, source_target_pairs={{0,8},{2,10},{4,12},{6,14},{8,0},{10,2},{12,4},{14,6},{17,25},{19,... | collective-permute-start | bytes 1572872 | tf_op jit(solution)/shard_map/ppermute | solution.py:479
  73.3 17.4 %copy-start.2 = (bf16[1024,1024]{1,0:T(8,128)(2,1)S(1)}, bf16[1024,1024]{1,0:T(8,128)(2,1)}, u32[]{:S(2)}) copy-start(bf16[1024,1024]{1,0:T(8,128)(2,1)} %pad_maximum_fusion.refs_4_) | copy-start | bytes 6291460
  93.4 3.1 %collective-permute-start.12 = (bf16[256,1024]{1,0:T(8,128)(2,1)}, bf16[256,1024]{1,0:T(8,128)(2,1)S(1)}, u32[]{:S(2)}, u32[]{:S(2)}) collective-permute-start(bf16[256,1024]{1,0:T(8,128)(2,1)} %convolution_convert_fusion.3), channel_id=1, source_target_pairs={{0,1},{1,0},{2,3},{3,2},{4,5},{5,4},{6,7},{7,6},{8,9},{9,8},{10,11... | collective-permute-start | bytes 1572872 | tf_op jit(solution)/shard_map/ppermute | solution.py:479
  97.5 14.3 %collective-permute-start.14 = (bf16[256,1024]{1,0:T(8,128)(2,1)}, bf16[256,1024]{1,0:T(8,128)(2,1)}, u32[]{:S(2)}, u32[]{:S(2)}) collective-permute-start(bf16[256,1024]{1,0:T(8,128)(2,1)} %add_convert_fusion), channel_id=1, source_target_pairs={{0,8},{1,9},{2,10},{3,11},{4,12},{5,13},{6,14},{7,15},{8,0},{9,1},... | collective-permute-start | bytes 1572872 | tf_op jit(solution)/shard_map/ppermute | solution.py:479
  103.8 8.0 %collective-permute-start.13 = (bf16[256,1024]{1,0:T(8,128)(2,1)}, bf16[256,1024]{1,0:T(8,128)(2,1)}, u32[]{:S(2)}, u32[]{:S(2)}) collective-permute-start(bf16[256,1024]{1,0:T(8,128)(2,1)} %convolution_convert_fusion.2), channel_id=1, source_target_pairs={{0,1},{1,0},{2,3},{3,2},{4,5},{5,4},{6,7},{7,6},{8,9},{9,8},{10,11... | collective-permute-start | bytes 1572872 | tf_op jit(solution)/shard_map/ppermute | solution.py:479
  104.9 21.0 %copy-start.6 = (bf16[256,1024]{1,0:T(8,128)(2,1)}, bf16[256,1024]{1,0:T(8,128)(2,1)S(1)}, u32[]{:S(2)}) copy-start(bf16[256,1024]{1,0:T(8,128)(2,1)S(1)} %broadcast_select_fusion.1) | copy-start | bytes 1572868
  104.9 14.5 %collective-permute-start.15 = (bf16[2,256,512]{2,1,0:T(8,128)(2,1)}, bf16[2,256,512]{2,1,0:T(8,128)(2,1)S(1)}, u32[]{:S(2)}, u32[]{:S(2)}) collective-permute-start(bf16[2,256,512]{2,1,0:T(8,128)(2,1)} %dynamic-slice_bitcast_fusion.1), channel_id=1, source_target_pairs={{0,2},{1,3},{2,0},{3,1},{4,6},{5,7},{6,4},{7,5},{8,10},{9,11},{10,... | collective-permute-start | bytes 1572872 | tf_op jit(solution)/shard_map/ppermute | solution.py:479
  106.5 17.6 %collective-permute-start.16 = (bf16[2,256,512]{2,1,0:T(8,128)(2,1)}, bf16[2,256,512]{2,1,0:T(8,128)(2,1)S(1)}, u32[]{:S(2)}, u32[]{:S(2)}) collective-permute-start(bf16[2,256,512]{2,1,0:T(8,128)(2,1)} %dynamic-slice_bitcast_fusion), channel_id=1, source_target_pairs={{0,4},{1,5},{2,6},{3,7},{4,0},{5,1},{6,2},{7,3},{8,12},{9,13},{10,... | collective-permute-start | bytes 1572872 | tf_op jit(solution)/shard_map/ppermute | solution.py:479
  125.1 0.7 collective-permute-start.19
  127.1 13.2 %collective-permute-start.20 = (bf16[512,1024]{1,0:T(8,128)(2,1)}, bf16[512,1024]{1,0:T(8,128)(2,1)}, u32[]{:S(2)}, u32[]{:S(2)}) collective-permute-start(bf16[512,1024]{1,0:T(8,128)(2,1)} %pad_maximum_fusion.2), channel_id=1, source_target_pairs={{0,1},{1,0},{2,3},{3,2},{4,5},{5,4},{6,7},{7,6},{8,9},{9,8},{10,11... | collective-permute-start | bytes 3145736 | tf_op jit(solution)/shard_map/ppermute | solution.py:479
  135.9 9.7 %collective-permute-start.18 = (bf16[256,512]{1,0:T(8,128)(2,1)}, bf16[256,512]{1,0:T(8,128)(2,1)}, u32[]{:S(2)}, u32[]{:S(2)}) collective-permute-start(bf16[256,512]{1,0:T(8,128)(2,1)} %dynamic-slice_bitcast_fusion.4), channel_id=1, source_target_pairs={{0,2},{1,3},{2,0},{3,1},{4,6},{5,7},{6,4},{7,5},{8,10},{9,11},{10,... | collective-permute-start | bytes 786440 | tf_op jit(solution)/shard_map/ppermute | solution.py:479
  136.5 40.1 %all-to-all-start = ((bf16[32,16,1152]{2,1,0:T(8,128)(2,1)}), bf16[32,16,1152]{2,1,0:T(8,128)(2,1)S(1)}, u32[]{:S(2)}, u32[]{:S(2)}) async-start(bf16[32,16,1152]{2,1,0:T(8,128)(2,1)} %bitcast.21), calls=%async_computation | async-start | bytes 2359296 | tf_op jit(solution)/shard_map/all_to_all | solution.py:401
  143.2 16.6 %collective-permute-start.21 = (bf16[256,512]{1,0:T(8,128)(2,1)}, bf16[256,512]{1,0:T(8,128)(2,1)S(1)}, u32[]{:S(2)}, u32[]{:S(2)}) collective-permute-start(bf16[256,512]{1,0:T(8,128)(2,1)} %broadcast_select_fusion.3), channel_id=1, source_target_pairs={{0,4},{1,5},{2,6},{3,7},{4,0},{5,1},{6,2},{7,3},{8,12},{9,13},{10,... | collective-permute-start | bytes 786440 | tf_op jit(solution)/shard_map/ppermute | solution.py:479
  144.8 22.0 %collective-permute-start.17 = (bf16[256,512]{1,0:T(8,128)(2,1)S(1)}, bf16[256,512]{1,0:T(8,128)(2,1)S(1)}, u32[]{:S(2)}, u32[]{:S(2)}) collective-permute-start(bf16[256,512]{1,0:T(8,128)(2,1)S(1)} %dynamic-slice_bitcast_fusion.5), channel_id=1, source_target_pairs={{0,4},{1,5},{2,6},{3,7},{4,0},{5,1},{6,2},{7,3},{8,12},{9,13},{10,... | collective-permute-start | bytes 786440 | tf_op jit(solution)/shard_map/ppermute | solution.py:479
  159.9 7.0 %collective-permute-start.22 = (bf16[256,256]{1,0:T(8,128)(2,1)S(1)}, bf16[256,256]{1,0:T(8,128)(2,1)S(1)}, u32[]{:S(2)}, u32[]{:S(2)}) collective-permute-start(bf16[256,256]{1,0:T(8,128)(2,1)S(1)} %broadcast_select_fusion.10), channel_id=1, source_target_pairs={{0,2},{1,3},{2,0},{3,1},{4,6},{5,7},{6,4},{7,5},{8,10},{9,11},{10,... | collective-permute-start | bytes 393224 | tf_op jit(solution)/shard_map/ppermute | solution.py:479
  167.0 8.8 %collective-permute-start.26 = (bf16[128,256]{1,0:T(8,128)(2,1)S(1)}, bf16[128,256]{1,0:T(8,128)(2,1)S(1)}, u32[]{:S(2)}, u32[]{:S(2)}) collective-permute-start(bf16[128,256]{1,0:T(8,128)(2,1)S(1)} %get-tuple-element.140), channel_id=1, source_target_pairs={{0,1},{1,3},{2,9},{3,11},{4,17},{5,19},{6,25},{7,27},{8,5},{9,7},{... | collective-permute-start | bytes 196616 | tf_op jit(solution)/shard_map/ppermute | solution.py:479
  167.1 8.8 %collective-permute-start.25 = (bf16[128,256]{1,0:T(8,128)(2,1)S(1)}, bf16[128,256]{1,0:T(8,128)(2,1)S(1)}, u32[]{:S(2)}, u32[]{:S(2)}) collective-permute-start(bf16[128,256]{1,0:T(8,128)(2,1)S(1)} %get-tuple-element.139), channel_id=1, source_target_pairs={{0,0},{1,2},{2,8},{3,10},{4,16},{5,18},{6,24},{7,26},{8,4},{9,6},{... | collective-permute-start | bytes 196616 | tf_op jit(solution)/shard_map/ppermute | solution.py:479
  168.5 13.4 %collective-permute-start.23 = (bf16[128,1024]{1,0:T(8,128)(2,1)}, bf16[128,1024]{1,0:T(8,128)(2,1)}, u32[]{:S(2)}, u32[]{:S(2)}) collective-permute-start(bf16[128,1024]{1,0:T(8,128)(2,1)} %get-tuple-element.128), channel_id=1, source_target_pairs={{0,0},{1,8},{2,2},{3,10},{4,4},{5,12},{6,6},{7,14},{8,16},{9,24},{... | collective-permute-start | bytes 786440 | tf_op jit(solution)/shard_map/ppermute | solution.py:479
  172.1 16.2 %collective-permute-start.24 = (bf16[128,1024]{1,0:T(8,128)(2,1)S(1)}, bf16[128,1024]{1,0:T(8,128)(2,1)}, u32[]{:S(2)}, u32[]{:S(2)}) collective-permute-start(bf16[128,1024]{1,0:T(8,128)(2,1)S(1)} %get-tuple-element.127), channel_id=1, source_target_pairs={{0,1},{1,9},{2,3},{3,11},{4,5},{5,13},{6,7},{7,15},{8,17},{9,25},{... | collective-permute-start | bytes 786440 | tf_op jit(solution)/shard_map/ppermute | solution.py:479
  (20 other events, 89.0 us)
